TPU v7x, 512 devices: a whole 4x4x16 slice. The times are simulated.
512 devices in a mesh: replica: 64 (over z_lo, x, core), tensor: 8 (over z_hi, y).
Axes of the slice: x: 4, y: 4, z: 16 (z_hi: 2, z_lo: 8; z = z_hi * 8 + z_lo), core: 2. Of those that a mesh axis runs over, the one named last changes fastest.
Arguments:
- tokens: bfloat16 [16384, 4096], P('replica', 'tensor'), may hold values from -6 to 6
- norm_gain: bfloat16 [64, 4096], P('replica', 'tensor'), may hold values from 0.5 to 1.5
- key_weight: bfloat16 [64, 4096, 1024], P('replica', None, 'tensor'), may hold values from -0.09375 to 0.09375
- value_weight: bfloat16 [64, 4096, 1024], P('replica', None, 'tensor'), may hold values from -0.09375 to 0.09375
- key_cotangent: bfloat16 [16384, 1024], P('replica', 'tensor'), may hold values from -6 to 6
- value_cotangent: bfloat16 [16384, 1024], P('replica', 'tensor'), may hold values from -6 to 6
- step_index: int32 [1], replicated, may hold values from 0 to 999
Outputs:
- mixed_key: bfloat16 [64, 4096, 1024], P('replica', None, 'tensor')
- mixed_value: bfloat16 [64, 4096, 1024], P('replica', None, 'tensor')
- mixed_gain: bfloat16 [64, 4096], P('replica', 'tensor')
- input_grad: bfloat16 [16384, 4096], P('replica', 'tensor')
Inputs may be any that keep to these rules, and one draw needn't show every extreme that they name: `step_index`: one training step index, the same for all replicas.
All inputs are finite; a program needn't handle non-finite values.
Results may differ from a plain program's by a relative error of at most 0.017.
Values may be sent and summed in bfloat16 or wider, within the bound.
No kernel may reach another device: no remote copies, remote signals or barrier semaphores. Data moves between devices by JAX's collectives and lax.ppermute only.
A program may use at most 64 MiB of HBM per device.

v0:
```python
import jax
import jax.numpy as jnp
from jax import lax
from jax.sharding import PartitionSpec as P

D = 4096
TOK = 256


lr_gain = 0.01
eps = 1e-05


def for_sending(shard):
    return jax.tree.map(lambda a: a.astype(jnp.bfloat16) if a.dtype == jnp.float32 else a, shard)


def shifted(shard, axis, by):
    length = lax.axis_size(axis)
    return lax.ppermute(shard, axis, [(i, (i + by) % length) for i in range(length)])


def fetch_updated(values, level, levels):

    def mover(offset):

        def moved(items):
            return jax.tree.map(
                lambda part, own: part.astype(own.dtype),
                shifted(for_sending(items), "replica", -offset),
                items,
            )

        return moved

    return lax.switch(level, [mover(2**j) for j in range(levels)], values)


def apply_step(weight, update, rate):
    return lax.optimization_barrier(
        (weight.astype(jnp.float32) - rate * update.astype(jnp.float32)).astype(jnp.bfloat16)
    )


def average_pair(mine, theirs):
    return ((mine.astype(jnp.float32) + theirs.astype(jnp.float32)) * 0.5).astype(jnp.bfloat16)


def per_device(
    tokens, norm_gain, key_weight, value_weight, key_cotangent, value_cotangent, step_index
):
    lr_weight = 0.25 / TOK
    levels = lax.axis_size("replica").bit_length() - 1
    level = jnp.mod(step_index[0], levels)
    xf = tokens.astype(jnp.float32)
    gf = norm_gain[0].astype(jnp.float32)
    squares = lax.psum(jnp.sum(xf * xf, axis=1), "tensor")
    rs = lax.rsqrt(squares[:, None] / D + eps)
    normed = (xf * rs * gf[None, :]).astype(jnp.bfloat16)
    cotangents = jnp.concatenate([key_cotangent, value_cotangent], axis=1)
    steps_both = jnp.dot(
        lax.all_gather(normed, "tensor", axis=1, tiled=True).T,
        cotangents,
        preferred_element_type=jnp.float32,
    )
    width = key_cotangent.shape[1]
    key_step = lax.optimization_barrier(steps_both[:, :width].astype(jnp.bfloat16))
    value_step = lax.optimization_barrier(steps_both[:, width:].astype(jnp.bfloat16))
    partial_grads = jnp.einsum(
        "tc,dc->td", key_cotangent, key_weight[0], preferred_element_type=jnp.float32
    )
    partial_grads = partial_grads + jnp.einsum(
        "tc,dc->td", value_cotangent, value_weight[0], preferred_element_type=jnp.float32
    )
    normed_grad = lax.psum_scatter(
        partial_grads.astype(jnp.bfloat16), "tensor", scatter_dimension=1, tiled=True
    ).astype(jnp.float32)
    gain_step = lax.optimization_barrier(
        jnp.sum(normed_grad * xf * rs, axis=0).astype(jnp.bfloat16)
    )
    centre = lax.psum(jnp.sum(normed_grad * gf[None, :] * xf, axis=1), "tensor")[:, None] / D
    input_grad = (rs * gf[None, :] * normed_grad - xf * rs * rs * rs * centre).astype(jnp.bfloat16)
    new_key = apply_step(key_weight, key_step[None], lr_weight)
    new_value = apply_step(value_weight, value_step[None], lr_weight)
    new_gain = apply_step(norm_gain, gain_step[None], lr_gain)
    other_key, other_value, other_gain = fetch_updated(
        (new_key, new_value, new_gain), level, levels
    )
    mixed_key = average_pair(new_key, other_key)
    mixed_value = average_pair(new_value, other_value)
    mixed_gain = average_pair(new_gain, other_gain)
    return (mixed_key, mixed_value, mixed_gain, input_grad)


def solution(mesh):
    return jax.shard_map(
        per_device,
        mesh=mesh,
        in_specs=(
            P("replica", "tensor"),
            P("replica", "tensor"),
            P("replica", None, "tensor"),
            P("replica", None, "tensor"),
            P("replica", "tensor"),
            P("replica", "tensor"),
            P(),
        ),
        out_specs=(
            P("replica", None, "tensor"),
            P("replica", None, "tensor"),
            P("replica", "tensor"),
            P("replica", "tensor"),
        ),
        check_vma=False,
    )
```

profile of v0, /device:TPU:1, one launch (start us, length us, event | category | flops | bytes accessed | tf_op | source)
XLA Modules:
  0.0 427.1 jit_solution(11616412554249824301)
XLA Ops:
  7.2 0.0 copy-start.3
  7.2 0.0 copy-start
  7.2 0.0 reduce-scatter.2.cloned.1.call-start
  7.2 2.0 fusion.8
  9.3 0.0 copy-done.3
  9.3 0.0 copy-done
  9.3 2.1 fusion
  11.4 0.0 copy-start.5
  11.4 0.0 copy-start.2
  11.4 0.0 copy-start.4
  11.4 0.0 reduce-scatter.2.cloned.1.call-update
  11.4 0.0 all-gather.2.cloned.1.call-start
  11.5 0.6 copy-done.5
  12.1 0.3 copy-done.2
  12.3 0.1 fusion.17
  12.5 47.1 %psum.14 = f32[256]{0:T(256)S(1)} all-reduce(f32[256]{0:T(256)S(1)} %fusion.17), channel_id=1, replica_groups=mesh['replica'=64,'tensor'=8] {'tensor'}, use_global_device_ids=true, to_apply=%region_1.2 | all-reduce | flops 256 | bytes 2048 | tf_op jit(solution)/shard_map/psum | solution.py:57
  59.6 103.5 %reduce-scatter.2.cloned.1.call-done = bf16[256,512]{1,0:T(8,128)(2,1)} async-done(((bf16[256,4096]{1,0:T(8,128)(2,1)}), bf16[256,512]{1,0:T(8,128)(2,1)}) %reduce-scatter.2.cloned.1.call-update) | async-done | bytes 262160 | tf_op jit(solution)/shard_map/reduce_scatter | solution.py:75
  163.1 1.2 fusion.20
  164.3 30.5 %psum.15 = f32[256]{0:T(256)S(1)} all-reduce(f32[256]{0:T(256)S(1)} %get-tuple-element.91), channel_id=1, replica_groups=mesh['replica'=64,'tensor'=8] {'tensor'}, use_global_device_ids=true, to_apply=%region_11.12 | all-reduce | flops 256 | bytes 2048 | tf_op jit(solution)/shard_map/psum | solution.py:81
  194.8 2.0 fusion.16
  196.8 0.0 all-gather.2.cloned.1.call-update
  197.5 121.2 %all-gather.2.cloned.1.call-done = bf16[256,4096]{1,0:T(8,128)(2,1)} async-done(((bf16[256,512]{1,0:T(8,128)(2,1)}), bf16[256,4096]{1,0:T(8,128)(2,1)}) %all-gather.2.cloned.1.call-update) | async-done | bytes 2097168 | tf_op jit(solution)/shard_map/all_gather | solution.py:62
  318.7 0.0 copy-done.4
  318.7 2.4 convolution_convert_fusion
  321.1 0.1 fusion.27
  321.2 0.0 copy-start.1
  321.2 0.3 fusion.5
  321.6 0.9 copy-done.1
  322.4 0.3 fusion.6
  322.8 92.7 %conditional.4 = (bf16[1,4096,128]{2,1,0:T(8,128)(2,1)}, bf16[1,4096,128]{2,1,0:T(8,128)(2,1)}, bf16[1,512]{1,0:T(2,128)(2,1)}) conditional(s32[]{:T(128)} %clamp.3, (bf16[1,4096,128]{2,1,0:T(8,128)(2,1)S(1)}, bf16[1,4096,128]{2,1,0:T(8,128)(2,1)S(1)}, bf16[1,512]{1,0:T(2,128)(2,1)S(1)}) %tuple.82, ...), branch_computations={%region_4.5_spmd, %region_5.6_spmd, %region_6.7_spmd, %region_7.8_... | conditional | bytes 8392848
  322.8 4.4 %collective-permute-start.12 = (bf16[1,4096,128]{2,1,0:T(8,128)(2,1)S(1)}, bf16[1,4096,128]{2,1,0:T(8,128)(2,1)}, u32[]{:S(2)}, u32[]{:S(2)}) collective-permute-start(bf16[1,4096,128]{2,1,0:T(8,128)(2,1)S(1)} %get-tuple-element.66), channel_id=1, source_target_pairs={{0,384},{8,392},{16,400},{24,408},{32,416},{40,424},{48,432},{56,4... | collective-permute-start | bytes 3145736 | tf_op jit(solution)/shard_map/cond/branch_4_fun/ppermute | solution.py:20
  327.2 1.9 collective-permute-start.13
  329.1 1.9 collective-permute-start.14
  331.1 84.4 %collective-permute-done.14 = bf16[1,512]{1,0:T(2,128)(2,1)} collective-permute-done((bf16[1,512]{1,0:T(2,128)(2,1)S(1)}, bf16[1,512]{1,0:T(2,128)(2,1)}, u32[]{:S(2)}, u32[]{:S(2)}) %collective-permute-start.14) | collective-permute-done | bytes 1056 | tf_op jit(solution)/shard_map/cond/branch_4_fun/ppermute | solution.py:20
  415.5 0.0 collective-permute-done.12
  415.5 0.0 collective-permute-done.13
  415.5 1.2 fusion.25
  416.7 3.5 fusion.2
  (5 shorter events, 0.0 us)
Async XLA Ops:
  7.2 2.1 copy-start.3
  7.2 2.1 copy-start
  7.2 155.9 %reduce-scatter.2.cloned.1.call-start = ((), (), s32[]{:S(2)}) async-start(), calls=%async_computation.2 | async-start | bytes 2359296 | tf_op jit(solution)/shard_map/reduce_scatter | solution.py:75
  11.4 0.7 copy-start.5
  11.4 1.0 copy-start.2
  11.4 307.3 %copy-start.4 = (bf16[256,128]{1,0:T(8,128)(2,1)S(1)}, bf16[256,128]{1,0:T(8,128)(2,1)}, u32[]{:S(2)}) copy-start(bf16[256,128]{1,0:T(8,128)(2,1)} %param.17) | copy-start | bytes 196612
  11.4 307.3 %all-gather.2.cloned.1.call-start = ((), (), s32[]{:S(2)}) async-start(), calls=%async_computation.1 | async-start | bytes 2359296 | tf_op jit(solution)/shard_map/all_gather | solution.py:62
  321.2 1.2 copy-start.1
  322.8 92.7 %collective-permute-start.12 = (bf16[1,4096,128]{2,1,0:T(8,128)(2,1)S(1)}, bf16[1,4096,128]{2,1,0:T(8,128)(2,1)}, u32[]{:S(2)}, u32[]{:S(2)}) collective-permute-start(bf16[1,4096,128]{2,1,0:T(8,128)(2,1)S(1)} %get-tuple-element.66), channel_id=1, source_target_pairs={{0,384},{8,392},{16,400},{24,408},{32,416},{40,424},{48,432},{56,4... | collective-permute-start | bytes 3145736 | tf_op jit(solution)/shard_map/cond/branch_4_fun/ppermute | solution.py:20
  327.2 88.3 %collective-permute-start.13 = (bf16[1,4096,128]{2,1,0:T(8,128)(2,1)S(1)}, bf16[1,4096,128]{2,1,0:T(8,128)(2,1)}, u32[]{:S(2)}, u32[]{:S(2)}) collective-permute-start(bf16[1,4096,128]{2,1,0:T(8,128)(2,1)S(1)} %get-tuple-element.67), channel_id=1, source_target_pairs={{0,384},{8,392},{16,400},{24,408},{32,416},{40,424},{48,432},{56,4... | collective-permute-start | bytes 3145736 | tf_op jit(solution)/shard_map/cond/branch_4_fun/ppermute | solution.py:20
  329.1 86.3 %collective-permute-start.14 = (bf16[1,512]{1,0:T(2,128)(2,1)S(1)}, bf16[1,512]{1,0:T(2,128)(2,1)}, u32[]{:S(2)}, u32[]{:S(2)}) collective-permute-start(bf16[1,512]{1,0:T(2,128)(2,1)S(1)} %get-tuple-element.68), channel_id=1, source_target_pairs={{0,384},{8,392},{16,400},{24,408},{32,416},{40,424},{48,432},{56,4... | collective-permute-start | bytes 3080 | tf_op jit(solution)/shard_map/cond/branch_4_fun/ppermute | solution.py:20
Sparse Core Ops, SparseCore 0:
  12.7 150.3 reduce-scatter.1
  197.0 121.6 all-gather.1
where the time goes:
time: 429 us; the launch traced here: 427 us
  waiting for transfers between devices  309 us (72%)
  blocking collectives  77.7 us (18%)
  between operations  14.8 us (3%)
  other arithmetic  8.81 us (2%)
  starting transfers between devices  8.3 us (2%)
  matrix products  6.48 us (2%)
    all_gather x1, waiting for transfers between devices, per_device(): lax.all_gather(normed, 'tensor', axis=1, tiled=True)  121 us
    reduce_scatter x1, waiting for transfers between devices, per_device(): lax.psum_scatter(partial_grads.astype(jnp.bfloat16), 'tensor', scatter_di...  103 us
    ppermute x3, waiting for transfers between devices, shifted(): lax.ppermute(shard, axis, [(i, (i + by) % length) for i in range(length)])  84.4 us
    psum x1, blocking collectives, per_device(): squares = lax.psum(jnp.sum(xf * xf, axis=1), 'tensor')  47.1 us
    psum x1, blocking collectives, per_device(): lax.psum(jnp.sum(normed_grad * gf[None, :] * xf, axis=1), 'tensor')[:, None]  30.5 us
  transfers between devices with their start and end apart: 5, of which 3 were waited for; matrix products, arithmetic and copies ran while one was open for 0% of the time, Pallas kernels for 0%

commit v1 on v0

v1 whole, which is shorter than its diff:
```python
import functools

import jax
import jax.numpy as jnp
from jax import lax
from jax.experimental import pallas as pl
from jax.experimental.pallas import tpu as pltpu
from jax.sharding import PartitionSpec as P

LR_GAIN = 0.01
EPS = 1e-05
PAD = 16
F32 = jnp.float32
BF16 = jnp.bfloat16
VMEM = pl.BlockSpec(memory_space=pltpu.VMEM)


def call(body, out_shape, flops, nbytes, count):
    return pl.pallas_call(
        body,
        out_shape=out_shape,
        in_specs=[VMEM] * count,
        out_specs=jax.tree.map(lambda _: VMEM, out_shape),
        compiler_params=pltpu.CompilerParams(vmem_limit_bytes=48 * 2**20),
        cost_estimate=pl.CostEstimate(flops=flops, bytes_accessed=nbytes, transcendentals=0),
    )


def partials_kernel(ny, ck, cv, wk, wv, far, near):
    half = lax.axis_index("tensor") // ny
    cols = far.shape[2]
    c = jnp.concatenate([ck[...], cv[...]], axis=1)
    for out, side in ((far, 1 - half), (near, half)):
        for y in range(ny):
            at = pl.ds(pl.multiple_of((side * ny + y) * cols, cols), cols)
            w = jnp.concatenate([wk[0, at, :], wv[0, at, :]], axis=1)
            out[y] = lax.dot_general(c, w, (((1,), (1,)), ((), ())), preferred_element_type=F32).astype(BF16)


def weights_kernel(ny, lr, eps, *refs):
    blocks, (ck, cv, wk, wv), (nk, nv, rs_out) = refs[:-7], refs[-7:-3], refs[-3:]
    tok = ck.shape[0]
    cols = blocks[0].shape[1]
    width = ck.shape[1]
    me = lax.axis_index("tensor")
    half, y = me // ny, me % ny
    squares = jnp.zeros((tok, 1), F32)
    for b in blocks:
        x = b[:tok].astype(F32)
        squares = squares + jnp.sum(x * x, axis=1, keepdims=True)
    rs = lax.rsqrt(squares / (cols * len(blocks)) + eps)
    rs_out[...] = rs
    c = jnp.concatenate([ck[...], cv[...]], axis=1)
    for i, b in enumerate(blocks):
        side = half if i < ny else 1 - half
        owner = side * ny + (y + (ny - i % ny)) % ny
        at = pl.ds(pl.multiple_of(owner * cols, cols), cols)
        g = b[tok : tok + 1].astype(F32)
        normed = (b[:tok].astype(F32) * rs * g).astype(BF16)
        step = lax.dot_general(normed, c, (((0,), (0,)), ((), ())), preferred_element_type=F32)
        step = step.astype(BF16).astype(F32)
        nk[0, at, :] = (wk[0, at, :].astype(F32) - lr * step[:, :width]).astype(BF16)
        nv[0, at, :] = (wv[0, at, :].astype(F32) - lr * step[:, width:]).astype(BF16)


def centre_kernel(ny, *refs):
    blocks, (far, near), out = refs[:-3], refs[-3:-1], refs[-1]
    tok = far.shape[1]
    cols = blocks[0].shape[1]
    y = lax.axis_index("tensor") % ny
    total = jnp.zeros((tok, 128), F32)
    for i, b in enumerate(blocks):
        src = near if i < ny else far
        p = src[(y + (ny - i % ny)) % ny].astype(F32)
        v = p * b[tok : tok + 1].astype(F32) * b[:tok].astype(F32)
        for j in range(0, cols, 128):
            total = total + v[:, j : j + 128]
    out[...] = jnp.sum(total.T, axis=0, keepdims=True)


def finish_kernel(features, near, far, x, gain, rs, centre, grad, new_gain):
    ng = near[...].astype(F32) + far[...].astype(F32)
    xf = x[...].astype(F32)
    g = gain[...].astype(F32)
    r = rs[...]
    mean = jnp.broadcast_to(centre[...] / features, (128, centre.shape[1])).T[:, :1]
    step = jnp.sum(ng * xf * r, axis=0, keepdims=True).astype(BF16).astype(F32)
    new_gain[...] = (g - LR_GAIN * step).astype(BF16)
    grad[...] = (r * g * ng - xf * (r * r * r * mean)).astype(BF16)


def average_pair(mine, theirs):
    return ((mine.astype(F32) + theirs.astype(F32)) * 0.5).astype(BF16)


def step_at(offset, nt, nr, tokens, norm_gain, key_weight, value_weight, key_cotangent, value_cotangent):
    ny = nt // 2
    tok, cols = tokens.shape
    width = key_cotangent.shape[1]
    features = cols * nt
    lr = 0.25 / tok

    def over_tensor(a, to):
        return lax.ppermute(a, "tensor", [(i, to(i)) for i in range(nt)])

    def over_z(a):
        return over_tensor(a, lambda i: (i + ny) % nt)

    def over_y(a, k):
        return over_tensor(a, lambda i: i // ny * ny + (i + k) % ny)

    def fetch(a):
        return lax.ppermute(a, "replica", [(i, (i - offset) % nr) for i in range(nr)])

    mine = jnp.concatenate([tokens, jnp.broadcast_to(norm_gain, (PAD, cols))], axis=0)
    other = over_z(mine)
    blocks = [mine] + [over_y(mine, k) for k in range(1, ny)]
    blocks += [other] + [over_y(other, k) for k in range(1, ny)]

    half_shape = jax.ShapeDtypeStruct((ny, tok, cols), BF16)
    far, near = call(
        functools.partial(partials_kernel, ny),
        (half_shape, half_shape),
        4 * tok * features * width,
        4 * features * width + 2 * tok * features,
        4,
    )(key_cotangent, value_cotangent, key_weight, value_weight)
    groups = [list(range(ny)), list(range(ny, nt))]

    def over_y_sum(a):
        return lax.psum_scatter(a, "tensor", scatter_dimension=0, axis_index_groups=groups)

    far_sum = over_y_sum(far)
    near_sum = over_y_sum(near)
    from_far = over_z(far_sum)

    weight_shape = jax.ShapeDtypeStruct(key_weight.shape, BF16)
    new_key, new_value, rs = call(
        functools.partial(weights_kernel, ny, lr, EPS),
        (weight_shape, weight_shape, jax.ShapeDtypeStruct((tok, 1), F32)),
        4 * tok * features * width,
        8 * features * width + 2 * tok * features,
        nt + 4,
    )(*blocks, key_cotangent, value_cotangent, key_weight, value_weight)
    other_key = fetch(new_key)
    other_value = fetch(new_value)

    centre = call(
        functools.partial(centre_kernel, ny),
        jax.ShapeDtypeStruct((1, tok), F32),
        4 * tok * features,
        4 * tok * features,
        nt + 2,
    )(*blocks, far, near)
    hop = 1
    while hop < nt:
        centre = centre + over_tensor(centre, lambda i: i ^ hop)
        hop *= 2

    input_grad, new_gain = call(
        functools.partial(finish_kernel, features),
        (jax.ShapeDtypeStruct((tok, cols), BF16), jax.ShapeDtypeStruct((1, cols), BF16)),
        10 * tok * cols,
        8 * tok * cols,
        6,
    )(near_sum, from_far, tokens, norm_gain, rs, centre)
    other_gain = fetch(new_gain)
    return (
        average_pair(new_key, other_key),
        average_pair(new_value, other_value),
        average_pair(new_gain, other_gain),
        input_grad,
    )


def per_device(*args):
    nt, nr = lax.axis_size("tensor"), lax.axis_size("replica")
    levels = nr.bit_length() - 1
    level = jnp.mod(args[-1][0], levels)
    branches = [functools.partial(step_at, 2**j, nt, nr) for j in range(levels)]
    return lax.switch(level, branches, *args[:-1])


def solution(mesh):
    rows, weights = P("replica", "tensor"), P("replica", None, "tensor")
    return jax.shard_map(
        per_device,
        mesh=mesh,
        in_specs=(rows, rows, weights, weights, rows, rows, P()),
        out_specs=(weights, weights, rows, rows),
        check_vma=False,
    )
```

time: 429 us -> 176 us (0.41)
  waiting for transfers between devices: 309 us -> 75.9 us
  blocking collectives: 77.7 us -> 0 us
  starting transfers between devices: 8.3 us -> 66.8 us
  Pallas kernels: 0 us -> 10.9 us
  matrix products: 6.48 us -> 0 us
  other arithmetic: 8.81 us -> 4.48 us
    all_gather x1 -> x0, waiting for transfers between devices: 121 us -> none  [per_device(): lax.all_gather(normed, 'tensor', axis=1, tiled=True)]
    reduce_scatter x1 -> x2, waiting for transfers between devices: 103 us -> 0.01 us  [over_y_sum(): lax.psum_scatter(a, 'tensor', scatter_dimension=0, axis_index_groups=groups)]
    psum x2 -> x0, blocking collectives: 77.7 us -> none  [the longest x1 47.1 us: per_device(): squares = lax.psum(jnp.sum(xf * xf, axis=1), 'tensor')]
    ppermute x3 -> x14, starting transfers between devices: 8.22 us -> 66.7 us  [the longest x11 52.8 us: over_tensor(): return lax.ppermute(a, 'tensor', [(i, to(i)) for i in range(nt)])]
    pallas_call x0 -> x4, Pallas kernels: none -> 10.9 us  [the longest x1 4.18 us: step_at(): call(functools.partial(weights_kernel, ny, lr, EPS), (weight_shape, weigh...]
    ppermute x3 -> x14, waiting for transfers between devices: 84.4 us -> 75.8 us  [the longest x11 75 us: over_tensor(): return lax.ppermute(a, 'tensor', [(i, to(i)) for i in range(nt)])]
    dot_general x3 -> x0, matrix products: 6.48 us -> none  [the longest x1 2.35 us: per_device(): jnp.dot(lax.all_gather(normed, 'tensor', axis=1, tiled=True).T, cotangent...]
  transfers between devices with their start and end apart: 5 -> 16, of which waited for: 3 -> 9; matrix products, arithmetic and copies ran while one was open for 0% -> 3% of each run, Pallas kernels for 0% -> 4%
where the time goes in v1:
time: 176 us
  waiting for transfers between devices  75.9 us (43%)
  starting transfers between devices  66.8 us (38%)
  between operations  14.7 us (8%)
  Pallas kernels  10.9 us (6%)
  other arithmetic  4.48 us (3%)
  local copies, waits for them, and re-layouts  2.77 us (2%)
    ppermute x11, waiting for transfers between devices, over_tensor(): return lax.ppermute(a, 'tensor', [(i, to(i)) for i in range(nt)])  75 us
    ppermute x11, starting transfers between devices, over_tensor(): return lax.ppermute(a, 'tensor', [(i, to(i)) for i in range(nt)])  52.8 us
    ppermute x3, starting transfers between devices, fetch(): lax.ppermute(a, 'replica', [(i, (i - offset) % nr) for i in range(nr)])  13.9 us
    convert_element_type x3, other arithmetic, average_pair(): return ((mine.astype(F32) + theirs.astype(F32)) * 0.5).astype(BF16)  4.43 us
    pallas_call x1, Pallas kernels, step_at(): call(functools.partial(weights_kernel, ny, lr, EPS), (weight_shape, weigh...  4.18 us
  transfers between devices with their start and end apart: 16, of which 9 were waited for; matrix products, arithmetic and copies ran while one was open for 3% of the time, Pallas kernels for 4%

profile of v1, /device:TPU:1, one launch (start us, length us, event | category | flops | bytes accessed | tf_op | source)
XLA Modules:
  0.0 175.7 jit_solution(6072270909570952884)
XLA Ops:
  7.8 160.1 %conditional.4 = (bf16[256,512]{1,0:T(8,128)(2,1)}, bf16[1,4096,128]{2,1,0:T(8,128)(2,1)}, bf16[1,4096,128]{2,1,0:T(8,128)(2,1)S(1)}, bf16[1,512]{1,0:T(2,128)(2,1)S(1)}) conditional(s32[]{:T(128)} %clamp.3, (bf16[256,128]{1,0:T(8,128)(2,1)}, bf16[256,128]{1,0:T(8,128)(2,1)}, bf16[1,4096,128]{2,1,0:T(8,128)(2,1)}, ...), branch_computations={%region_0.3_spmd, %region_3.6_spmd, %region_6.9_spmd, %region_9.12... | conditional | flops 1085050112 | bytes 51400520
  7.9 0.0 reduce-scatter.19.cloned.1.call-start
  7.9 3.4 %branch_1_fun.4 = (bf16[4,256,512]{2,1,0:T(8,128)(2,1)}, bf16[4,256,512]{2,1,0:T(8,128)(2,1)}) custom-call(bf16[256,128]{1,0:T(8,128)(2,1)} %get-tuple-element.105.ck.refs_8_, bf16[256,128]{1,0:T(8,128)(2,1)} %get-tuple-element.106.cv.refs_9_, bf16[1,4096,128]{2,1,0:T(8,128)(2,1)} %get-tuple-element.107.wk.refs_10_, ...), custom_call_target="tpu_custom_call" | custom-call | flops 536870912 | bytes 4194304 | tf_op jit(solution)/shard_map/cond/branch_1_fun/pallas_call | solution.py:121
  11.3 0.0 copy-start.32
  11.3 0.0 copy-start.8
  11.3 0.0 reduce-scatter.19.cloned.1.call-update
  11.4 0.0 copy-start.19
  11.4 0.0 copy-start.25
  11.4 0.0 reduce-scatter.17.cloned.1.call-start
  11.4 0.6 copy-done.32
  12.0 0.3 copy-done.8
  12.3 16.3 %collective-permute-start.18 = (bf16[272,512]{1,0:T(8,128)(2,1)S(1)}, bf16[272,512]{1,0:T(8,128)(2,1)S(1)}, u32[]{:S(2)}, u32[]{:S(2)}) collective-permute-start(bf16[272,512]{1,0:T(8,128)(2,1)S(1)} %pad_maximum_fusion.1.refs_0_), channel_id=1, source_target_pairs={{0,4},{1,5},{2,6},{3,7},{4,0},{5,1},{6,2},{7,3},{8,12},{9,13},{10,... | collective-permute-start | bytes 835592 | tf_op jit(solution)/shard_map/cond/branch_1_fun/ppermute | solution.py:104
  28.6 4.6 %collective-permute-start.17 = (bf16[272,512]{1,0:T(8,128)(2,1)S(1)}, bf16[272,512]{1,0:T(8,128)(2,1)S(1)}, u32[]{:S(2)}, u32[]{:S(2)}) collective-permute-start(bf16[272,512]{1,0:T(8,128)(2,1)S(1)} %pad_maximum_fusion.1.refs_0_), channel_id=1, source_target_pairs={{0,3},{1,0},{2,1},{3,2},{4,7},{5,4},{6,5},{7,6},{8,11},{9,8},{10,9... | collective-permute-start | bytes 835592 | tf_op jit(solution)/shard_map/cond/branch_1_fun/ppermute | solution.py:104
  33.2 2.3 %collective-permute-start.16 = (bf16[272,512]{1,0:T(8,128)(2,1)S(1)}, bf16[272,512]{1,0:T(8,128)(2,1)S(1)}, u32[]{:S(2)}, u32[]{:S(2)}) collective-permute-start(bf16[272,512]{1,0:T(8,128)(2,1)S(1)} %pad_maximum_fusion.1.refs_0_), channel_id=1, source_target_pairs={{0,2},{1,3},{2,0},{3,1},{4,6},{5,7},{6,4},{7,5},{8,10},{9,11},{10,... | collective-permute-start | bytes 835592 | tf_op jit(solution)/shard_map/cond/branch_1_fun/ppermute | solution.py:104
  35.5 2.6 %collective-permute-start.15 = (bf16[272,512]{1,0:T(8,128)(2,1)S(1)}, bf16[272,512]{1,0:T(8,128)(2,1)S(1)}, u32[]{:S(2)}, u32[]{:S(2)}) collective-permute-start(bf16[272,512]{1,0:T(8,128)(2,1)S(1)} %pad_maximum_fusion.1.refs_0_), channel_id=1, source_target_pairs={{0,1},{1,2},{2,3},{3,0},{4,5},{5,6},{6,7},{7,4},{8,9},{9,10},{10,1... | collective-permute-start | bytes 835592 | tf_op jit(solution)/shard_map/cond/branch_1_fun/ppermute | solution.py:104
  38.1 0.0 collective-permute-done.18.refs_4_
  38.1 3.9 %collective-permute-start.21 = (bf16[272,512]{1,0:T(8,128)(2,1)S(1)}, bf16[272,512]{1,0:T(8,128)(2,1)S(1)}, u32[]{:S(2)}, u32[]{:S(2)}) collective-permute-start(bf16[272,512]{1,0:T(8,128)(2,1)S(1)} %collective-permute-done.18.refs_4_), channel_id=1, source_target_pairs={{0,3},{1,0},{2,1},{3,2},{4,7},{5,4},{6,5},{7,6},{8,11},{9,8},{10,9... | collective-permute-start | bytes 835592 | tf_op jit(solution)/shard_map/cond/branch_1_fun/ppermute | solution.py:104
  42.0 3.3 %collective-permute-start.20 = (bf16[272,512]{1,0:T(8,128)(2,1)S(1)}, bf16[272,512]{1,0:T(8,128)(2,1)S(1)}, u32[]{:S(2)}, u32[]{:S(2)}) collective-permute-start(bf16[272,512]{1,0:T(8,128)(2,1)S(1)} %collective-permute-done.18.refs_4_), channel_id=1, source_target_pairs={{0,2},{1,3},{2,0},{3,1},{4,6},{5,7},{6,4},{7,5},{8,10},{9,11},{10,... | collective-permute-start | bytes 835592 | tf_op jit(solution)/shard_map/cond/branch_1_fun/ppermute | solution.py:104
  45.4 0.0 collective-permute-done.17.refs_3_
  45.4 1.9 %collective-permute-start.19 = (bf16[272,512]{1,0:T(8,128)(2,1)S(1)}, bf16[272,512]{1,0:T(8,128)(2,1)S(1)}, u32[]{:S(2)}, u32[]{:S(2)}) collective-permute-start(bf16[272,512]{1,0:T(8,128)(2,1)S(1)} %collective-permute-done.18.refs_4_), channel_id=1, source_target_pairs={{0,1},{1,2},{2,3},{3,0},{4,5},{5,6},{6,7},{7,4},{8,9},{9,10},{10,1... | collective-permute-start | bytes 835592 | tf_op jit(solution)/shard_map/cond/branch_1_fun/ppermute | solution.py:104
  47.3 0.0 reduce-scatter.17.cloned.1.call-update
  47.3 2.3 %collective-permute-done.16.refs_2_ = bf16[272,512]{1,0:T(8,128)(2,1)S(1)} collective-permute-done((bf16[272,512]{1,0:T(8,128)(2,1)S(1)}, bf16[272,512]{1,0:T(8,128)(2,1)S(1)}, u32[]{:S(2)}, u32[]{:S(2)}) %collective-permute-start.16) | collective-permute-done | bytes 278560 | tf_op jit(solution)/shard_map/cond/branch_1_fun/ppermute | solution.py:104
  49.7 7.5 %collective-permute-done.15.refs_1_ = bf16[272,512]{1,0:T(8,128)(2,1)S(1)} collective-permute-done((bf16[272,512]{1,0:T(8,128)(2,1)S(1)}, bf16[272,512]{1,0:T(8,128)(2,1)S(1)}, u32[]{:S(2)}, u32[]{:S(2)}) %collective-permute-start.15) | collective-permute-done | bytes 278560 | tf_op jit(solution)/shard_map/cond/branch_1_fun/ppermute | solution.py:104
  57.1 8.0 %collective-permute-done.21.refs_7_ = bf16[272,512]{1,0:T(8,128)(2,1)S(1)} collective-permute-done((bf16[272,512]{1,0:T(8,128)(2,1)S(1)}, bf16[272,512]{1,0:T(8,128)(2,1)S(1)}, u32[]{:S(2)}, u32[]{:S(2)}) %collective-permute-start.21) | collective-permute-done | bytes 278560 | tf_op jit(solution)/shard_map/cond/branch_1_fun/ppermute | solution.py:104
  65.1 0.0 collective-permute-done.20.refs_6_
  65.1 4.1 %collective-permute-done.19.refs_5_ = bf16[272,512]{1,0:T(8,128)(2,1)S(1)} collective-permute-done((bf16[272,512]{1,0:T(8,128)(2,1)S(1)}, bf16[272,512]{1,0:T(8,128)(2,1)S(1)}, u32[]{:S(2)}, u32[]{:S(2)}) %collective-permute-start.19) | collective-permute-done | bytes 278560 | tf_op jit(solution)/shard_map/cond/branch_1_fun/ppermute | solution.py:104
  69.2 0.0 copy-done.19
  69.2 0.0 copy-done.25
  69.2 4.2 %branch_1_fun.5 = (bf16[1,4096,128]{2,1,0:T(8,128)(2,1)}, bf16[1,4096,128]{2,1,0:T(8,128)(2,1)S(1)}, f32[256,1]{1,0:T(8,128)S(1)}) custom-call(bf16[272,512]{1,0:T(8,128)(2,1)S(1)} %pad_maximum_fusion.1.refs_0_, bf16[272,512]{1,0:T(8,128)(2,1)S(1)} %collective-permute-done.15.refs_1_, bf16[272,512]{1,0:T(8,128)(2,1)S(1)} %collective-permute-done.16.refs_2_, ...), custom_call_target="tpu_custom_call" | custom-call | flops 536870912 | bytes 6291456 | tf_op jit(solution)/shard_map/cond/branch_1_fun/pallas_call | solution.py:138
  73.4 9.5 %collective-permute-start.25 = (bf16[1,4096,128]{2,1,0:T(8,128)(2,1)}, bf16[1,4096,128]{2,1,0:T(8,128)(2,1)}, u32[]{:S(2)}, u32[]{:S(2)}) collective-permute-start(bf16[1,4096,128]{2,1,0:T(8,128)(2,1)} %get-tuple-element.115), channel_id=1, source_target_pairs={{0,496},{8,504},{16,0},{24,8},{32,16},{40,24},{48,32},{56,40},{64,... | collective-permute-start | bytes 3145736 | tf_op jit(solution)/shard_map/cond/branch_1_fun/ppermute | solution.py:113
  82.9 2.5 %collective-permute-start.26 = (bf16[1,4096,128]{2,1,0:T(8,128)(2,1)S(1)}, bf16[1,4096,128]{2,1,0:T(8,128)(2,1)}, u32[]{:S(2)}, u32[]{:S(2)}) collective-permute-start(bf16[1,4096,128]{2,1,0:T(8,128)(2,1)S(1)} %get-tuple-element.116), channel_id=1, source_target_pairs={{0,496},{8,504},{16,0},{24,8},{32,16},{40,24},{48,32},{56,40},{64,... | collective-permute-start | bytes 3145736 | tf_op jit(solution)/shard_map/cond/branch_1_fun/ppermute | solution.py:113
  85.4 2.3 %branch_1_fun.6 = f32[1,256]{1,0:T(1,128)S(1)} custom-call(bf16[272,512]{1,0:T(8,128)(2,1)S(1)} %pad_maximum_fusion.1.refs_0_, bf16[272,512]{1,0:T(8,128)(2,1)S(1)} %collective-permute-done.15.refs_1_, bf16[272,512]{1,0:T(8,128)(2,1)S(1)} %collective-permute-done.16.refs_2_, bf16[272,512]{1,0:T(8,128)(2,1)S(1)} %collective-permute-done.17.refs_3_, ...), custom_call_target="tpu_custom_call" | custom-call | flops 4194304 | bytes 4194304 | tf_op jit(solution)/shard_map/cond/branch_1_fun/pallas_call | solution.py:148
  87.7 1.9 %collective-permute-start.22 = (f32[1,256]{1,0:T(1,128)S(1)}, f32[1,256]{1,0:T(1,128)S(1)}, u32[]{:S(2)}, u32[]{:S(2)}) collective-permute-start(f32[1,256]{1,0:T(1,128)S(1)} %branch_1_fun.6), channel_id=1, source_target_pairs={{0,1},{1,0},{2,3},{3,2},{4,5},{5,4},{6,7},{7,6},{8,9},{9,8},{10,11... | collective-permute-start | bytes 3080 | tf_op jit(solution)/shard_map/cond/branch_1_fun/ppermute | solution.py:104
  89.7 2.8 %collective-permute-done.22 = f32[1,256]{1,0:T(1,128)S(1)} collective-permute-done((f32[1,256]{1,0:T(1,128)S(1)}, f32[1,256]{1,0:T(1,128)S(1)}, u32[]{:S(2)}, u32[]{:S(2)}) %collective-permute-start.22) | collective-permute-done | bytes 1056 | tf_op jit(solution)/shard_map/cond/branch_1_fun/ppermute | solution.py:104
  92.4 2.4 %collective-permute-start.23 = (f32[1,256]{1,0:T(1,128)S(1)}, f32[1,256]{1,0:T(1,128)S(1)}, u32[]{:S(2)}, u32[]{:S(2)}) collective-permute-start(f32[1,256]{1,0:T(1,128)S(1)} %add.105), channel_id=1, source_target_pairs={{0,2},{1,3},{2,0},{3,1},{4,6},{5,7},{6,4},{7,5},{8,10},{9,11},{10,... | collective-permute-start | bytes 3080 | tf_op jit(solution)/shard_map/cond/branch_1_fun/ppermute | solution.py:104
  94.8 3.4 %collective-permute-done.23 = f32[1,256]{1,0:T(1,128)S(1)} collective-permute-done((f32[1,256]{1,0:T(1,128)S(1)}, f32[1,256]{1,0:T(1,128)S(1)}, u32[]{:S(2)}, u32[]{:S(2)}) %collective-permute-start.23) | collective-permute-done | bytes 1056 | tf_op jit(solution)/shard_map/cond/branch_1_fun/ppermute | solution.py:104
  98.3 10.6 %collective-permute-start.24 = (f32[1,256]{1,0:T(1,128)S(1)}, f32[1,256]{1,0:T(1,128)S(1)}, u32[]{:S(2)}, u32[]{:S(2)}) collective-permute-start(f32[1,256]{1,0:T(1,128)S(1)} %add.106), channel_id=1, source_target_pairs={{0,4},{1,5},{2,6},{3,7},{4,0},{5,1},{6,2},{7,3},{8,12},{9,13},{10,... | collective-permute-start | bytes 3080 | tf_op jit(solution)/shard_map/cond/branch_1_fun/ppermute | solution.py:104
  108.9 28.3 %collective-permute-done.24 = f32[1,256]{1,0:T(1,128)S(1)} collective-permute-done((f32[1,256]{1,0:T(1,128)S(1)}, f32[1,256]{1,0:T(1,128)S(1)}, u32[]{:S(2)}, u32[]{:S(2)}) %collective-permute-start.24) | collective-permute-done | bytes 1056 | tf_op jit(solution)/shard_map/cond/branch_1_fun/ppermute | solution.py:104
  137.2 0.0 reduce-scatter.19.cloned.1.call-done
  137.2 0.0 copy-start.9
  137.2 3.0 %collective-permute-start.14 = (bf16[256,512]{1,0:T(8,128)(2,1)}, bf16[256,512]{1,0:T(8,128)(2,1)S(1)}, u32[]{:S(2)}, u32[]{:S(2)}) collective-permute-start(bf16[256,512]{1,0:T(8,128)(2,1)} %bitcast.20), channel_id=1, source_target_pairs={{0,4},{1,5},{2,6},{3,7},{4,0},{5,1},{6,2},{7,3},{8,12},{9,13},{10,... | collective-permute-start | bytes 786440 | tf_op jit(solution)/shard_map/cond/branch_1_fun/ppermute | solution.py:104
  140.2 0.0 collective-permute-done.25
  140.2 2.9 %multiply_convert_fusion.4 = bf16[1,4096,128]{2,1,0:T(8,128)(2,1)} fusion(bf16[1,4096,128]{2,1,0:T(8,128)(2,1)} %collective-permute-done.25, bf16[1,4096,128]{2,1,0:T(8,128)(2,1)} %get-tuple-element.115), kind=kLoop, calls=%fused_computation.5 | loop fusion | flops 2621440 | bytes 3145728 | tf_op jit(solution)/shard_map/cond/branch_0_fun/convert_element_type | solution.py:93
  143.1 0.0 reduce-scatter.17.cloned.1.call-done
  143.1 18.6 %collective-permute-done.14.far = bf16[256,512]{1,0:T(8,128)(2,1)S(1)} collective-permute-done((bf16[256,512]{1,0:T(8,128)(2,1)}, bf16[256,512]{1,0:T(8,128)(2,1)S(1)}, u32[]{:S(2)}, u32[]{:S(2)}) %collective-permute-start.14) | collective-permute-done | bytes 262176 | tf_op jit(solution)/shard_map/cond/branch_1_fun/ppermute | solution.py:104
  161.6 0.0 copy-done.9
  161.7 0.0 copy-start.1
  161.7 0.9 copy-done.1
  162.6 1.0 branch_1_fun.7
  163.6 1.9 %collective-permute-start.27 = (bf16[1,512]{1,0:T(2,128)(2,1)S(1)}, bf16[1,512]{1,0:T(2,128)(2,1)S(1)}, u32[]{:S(2)}, u32[]{:S(2)}) collective-permute-start(bf16[1,512]{1,0:T(2,128)(2,1)S(1)} %get-tuple-element.117), channel_id=1, source_target_pairs={{0,496},{8,504},{16,0},{24,8},{32,16},{40,24},{48,32},{56,40},{64,... | collective-permute-start | bytes 3080 | tf_op jit(solution)/shard_map/cond/branch_1_fun/ppermute | solution.py:113
  165.5 0.0 collective-permute-done.26
  165.5 1.6 multiply_convert_fusion.3
  167.1 0.8 collective-permute-done.27
  167.9 0.0 copy-start.30
  167.9 0.0 copy-start.37
  167.9 1.0 copy-done.30
  168.9 0.0 copy-done.37
  (7 shorter events, 0.1 us)
Async XLA Ops:
  7.9 129.3 %reduce-scatter.19.cloned.1.call-start = ((), (), s32[]{:S(2)}) async-start(), calls=%async_computation.15 | async-start | bytes 1310720 | tf_op jit(solution)/shard_map/cond/branch_1_fun/reduce_scatter | solution.py:131
  11.3 0.7 copy-start.32
  11.3 1.0 copy-start.8
  11.4 57.9 %copy-start.19 = (bf16[256,128]{1,0:T(8,128)(2,1)S(1)}, bf16[256,128]{1,0:T(8,128)(2,1)}, u32[]{:S(2)}) copy-start(bf16[256,128]{1,0:T(8,128)(2,1)} %get-tuple-element.105.ck.refs_8_) | copy-start | bytes 196612
  11.4 57.9 %copy-start.25 = (bf16[256,128]{1,0:T(8,128)(2,1)S(1)}, bf16[256,128]{1,0:T(8,128)(2,1)}, u32[]{:S(2)}) copy-start(bf16[256,128]{1,0:T(8,128)(2,1)} %get-tuple-element.106.cv.refs_9_) | copy-start | bytes 196612
  11.4 131.7 %reduce-scatter.17.cloned.1.call-start = ((), (), s32[]{:S(2)}) async-start(), calls=%async_computation.14 | async-start | bytes 1310720 | tf_op jit(solution)/shard_map/cond/branch_1_fun/reduce_scatter | solution.py:131
  12.3 25.8 %collective-permute-start.18 = (bf16[272,512]{1,0:T(8,128)(2,1)S(1)}, bf16[272,512]{1,0:T(8,128)(2,1)S(1)}, u32[]{:S(2)}, u32[]{:S(2)}) collective-permute-start(bf16[272,512]{1,0:T(8,128)(2,1)S(1)} %pad_maximum_fusion.1.refs_0_), channel_id=1, source_target_pairs={{0,4},{1,5},{2,6},{3,7},{4,0},{5,1},{6,2},{7,3},{8,12},{9,13},{10,... | collective-permute-start | bytes 835592 | tf_op jit(solution)/shard_map/cond/branch_1_fun/ppermute | solution.py:104
  28.6 16.8 %collective-permute-start.17 = (bf16[272,512]{1,0:T(8,128)(2,1)S(1)}, bf16[272,512]{1,0:T(8,128)(2,1)S(1)}, u32[]{:S(2)}, u32[]{:S(2)}) collective-permute-start(bf16[272,512]{1,0:T(8,128)(2,1)S(1)} %pad_maximum_fusion.1.refs_0_), channel_id=1, source_target_pairs={{0,3},{1,0},{2,1},{3,2},{4,7},{5,4},{6,5},{7,6},{8,11},{9,8},{10,9... | collective-permute-start | bytes 835592 | tf_op jit(solution)/shard_map/cond/branch_1_fun/ppermute | solution.py:104
  33.2 16.4 %collective-permute-start.16 = (bf16[272,512]{1,0:T(8,128)(2,1)S(1)}, bf16[272,512]{1,0:T(8,128)(2,1)S(1)}, u32[]{:S(2)}, u32[]{:S(2)}) collective-permute-start(bf16[272,512]{1,0:T(8,128)(2,1)S(1)} %pad_maximum_fusion.1.refs_0_), channel_id=1, source_target_pairs={{0,2},{1,3},{2,0},{3,1},{4,6},{5,7},{6,4},{7,5},{8,10},{9,11},{10,... | collective-permute-start | bytes 835592 | tf_op jit(solution)/shard_map/cond/branch_1_fun/ppermute | solution.py:104
  35.5 21.6 %collective-permute-start.15 = (bf16[272,512]{1,0:T(8,128)(2,1)S(1)}, bf16[272,512]{1,0:T(8,128)(2,1)S(1)}, u32[]{:S(2)}, u32[]{:S(2)}) collective-permute-start(bf16[272,512]{1,0:T(8,128)(2,1)S(1)} %pad_maximum_fusion.1.refs_0_), channel_id=1, source_target_pairs={{0,1},{1,2},{2,3},{3,0},{4,5},{5,6},{6,7},{7,4},{8,9},{9,10},{10,1... | collective-permute-start | bytes 835592 | tf_op jit(solution)/shard_map/cond/branch_1_fun/ppermute | solution.py:104
  38.1 27.0 %collective-permute-start.21 = (bf16[272,512]{1,0:T(8,128)(2,1)S(1)}, bf16[272,512]{1,0:T(8,128)(2,1)S(1)}, u32[]{:S(2)}, u32[]{:S(2)}) collective-permute-start(bf16[272,512]{1,0:T(8,128)(2,1)S(1)} %collective-permute-done.18.refs_4_), channel_id=1, source_target_pairs={{0,3},{1,0},{2,1},{3,2},{4,7},{5,4},{6,5},{7,6},{8,11},{9,8},{10,9... | collective-permute-start | bytes 835592 | tf_op jit(solution)/shard_map/cond/branch_1_fun/ppermute | solution.py:104
  42.0 23.1 %collective-permute-start.20 = (bf16[272,512]{1,0:T(8,128)(2,1)S(1)}, bf16[272,512]{1,0:T(8,128)(2,1)S(1)}, u32[]{:S(2)}, u32[]{:S(2)}) collective-permute-start(bf16[272,512]{1,0:T(8,128)(2,1)S(1)} %collective-permute-done.18.refs_4_), channel_id=1, source_target_pairs={{0,2},{1,3},{2,0},{3,1},{4,6},{5,7},{6,4},{7,5},{8,10},{9,11},{10,... | collective-permute-start | bytes 835592 | tf_op jit(solution)/shard_map/cond/branch_1_fun/ppermute | solution.py:104
  45.4 23.9 %collective-permute-start.19 = (bf16[272,512]{1,0:T(8,128)(2,1)S(1)}, bf16[272,512]{1,0:T(8,128)(2,1)S(1)}, u32[]{:S(2)}, u32[]{:S(2)}) collective-permute-start(bf16[272,512]{1,0:T(8,128)(2,1)S(1)} %collective-permute-done.18.refs_4_), channel_id=1, source_target_pairs={{0,1},{1,2},{2,3},{3,0},{4,5},{5,6},{6,7},{7,4},{8,9},{9,10},{10,1... | collective-permute-start | bytes 835592 | tf_op jit(solution)/shard_map/cond/branch_1_fun/ppermute | solution.py:104
  73.4 66.8 %collective-permute-start.25 = (bf16[1,4096,128]{2,1,0:T(8,128)(2,1)}, bf16[1,4096,128]{2,1,0:T(8,128)(2,1)}, u32[]{:S(2)}, u32[]{:S(2)}) collective-permute-start(bf16[1,4096,128]{2,1,0:T(8,128)(2,1)} %get-tuple-element.115), channel_id=1, source_target_pairs={{0,496},{8,504},{16,0},{24,8},{32,16},{40,24},{48,32},{56,40},{64,... | collective-permute-start | bytes 3145736 | tf_op jit(solution)/shard_map/cond/branch_1_fun/ppermute | solution.py:113
  82.9 82.6 %collective-permute-start.26 = (bf16[1,4096,128]{2,1,0:T(8,128)(2,1)S(1)}, bf16[1,4096,128]{2,1,0:T(8,128)(2,1)}, u32[]{:S(2)}, u32[]{:S(2)}) collective-permute-start(bf16[1,4096,128]{2,1,0:T(8,128)(2,1)S(1)} %get-tuple-element.116), channel_id=1, source_target_pairs={{0,496},{8,504},{16,0},{24,8},{32,16},{40,24},{48,32},{56,40},{64,... | collective-permute-start | bytes 3145736 | tf_op jit(solution)/shard_map/cond/branch_1_fun/ppermute | solution.py:113
  87.7 4.7 %collective-permute-start.22 = (f32[1,256]{1,0:T(1,128)S(1)}, f32[1,256]{1,0:T(1,128)S(1)}, u32[]{:S(2)}, u32[]{:S(2)}) collective-permute-start(f32[1,256]{1,0:T(1,128)S(1)} %branch_1_fun.6), channel_id=1, source_target_pairs={{0,1},{1,0},{2,3},{3,2},{4,5},{5,4},{6,7},{7,6},{8,9},{9,8},{10,11... | collective-permute-start | bytes 3080 | tf_op jit(solution)/shard_map/cond/branch_1_fun/ppermute | solution.py:104
  92.4 5.8 %collective-permute-start.23 = (f32[1,256]{1,0:T(1,128)S(1)}, f32[1,256]{1,0:T(1,128)S(1)}, u32[]{:S(2)}, u32[]{:S(2)}) collective-permute-start(f32[1,256]{1,0:T(1,128)S(1)} %add.105), channel_id=1, source_target_pairs={{0,2},{1,3},{2,0},{3,1},{4,6},{5,7},{6,4},{7,5},{8,10},{9,11},{10,... | collective-permute-start | bytes 3080 | tf_op jit(solution)/shard_map/cond/branch_1_fun/ppermute | solution.py:104
  98.3 38.9 %collective-permute-start.24 = (f32[1,256]{1,0:T(1,128)S(1)}, f32[1,256]{1,0:T(1,128)S(1)}, u32[]{:S(2)}, u32[]{:S(2)}) collective-permute-start(f32[1,256]{1,0:T(1,128)S(1)} %add.106), channel_id=1, source_target_pairs={{0,4},{1,5},{2,6},{3,7},{4,0},{5,1},{6,2},{7,3},{8,12},{9,13},{10,... | collective-permute-start | bytes 3080 | tf_op jit(solution)/shard_map/cond/branch_1_fun/ppermute | solution.py:104
  137.2 24.5 %copy-start.9 = (bf16[256,512]{1,0:T(8,128)(2,1)S(1)}, bf16[256,512]{1,0:T(8,128)(2,1)}, u32[]{:S(2)}) copy-start(bf16[256,512]{1,0:T(8,128)(2,1)} %get-tuple-element.111.x) | copy-start | bytes 786436
  137.2 24.4 %collective-permute-start.14 = (bf16[256,512]{1,0:T(8,128)(2,1)}, bf16[256,512]{1,0:T(8,128)(2,1)S(1)}, u32[]{:S(2)}, u32[]{:S(2)}) collective-permute-start(bf16[256,512]{1,0:T(8,128)(2,1)} %bitcast.20), channel_id=1, source_target_pairs={{0,4},{1,5},{2,6},{3,7},{4,0},{5,1},{6,2},{7,3},{8,12},{9,13},{10,... | collective-permute-start | bytes 786440 | tf_op jit(solution)/shard_map/cond/branch_1_fun/ppermute | solution.py:104
  161.7 1.0 copy-start.1
  163.6 4.3 %collective-permute-start.27 = (bf16[1,512]{1,0:T(2,128)(2,1)S(1)}, bf16[1,512]{1,0:T(2,128)(2,1)S(1)}, u32[]{:S(2)}, u32[]{:S(2)}) collective-permute-start(bf16[1,512]{1,0:T(2,128)(2,1)S(1)} %get-tuple-element.117), channel_id=1, source_target_pairs={{0,496},{8,504},{16,0},{24,8},{32,16},{40,24},{48,32},{56,40},{64,... | collective-permute-start | bytes 3080 | tf_op jit(solution)/shard_map/cond/branch_1_fun/ppermute | solution.py:113
  167.9 1.0 copy-start.30
  167.9 1.0 copy-start.37
Sparse Core Ops, SparseCore 0:
  12.3 44.4 reduce-scatter.18
  59.7 33.8 reduce-scatter.16

commit v2 on v1

v2 whole, which is shorter than its diff:
```python
import functools

import jax
import jax.numpy as jnp
from jax import lax
from jax.experimental import pallas as pl
from jax.experimental.pallas import tpu as pltpu
from jax.sharding import PartitionSpec as P

LR_GAIN = 0.01
EPS = 1e-05
PAD = 16
F32 = jnp.float32
BF16 = jnp.bfloat16
VMEM = pl.BlockSpec(memory_space=pltpu.VMEM)
ANY = pl.BlockSpec(memory_space=pl.ANY)
PARAMS = pltpu.CompilerParams(vmem_limit_bytes=48 * 2**20)


def call(body, out_shape, operands, flops, after=()):
    count = len(operands)

    def kernel(*refs):
        body(*refs[:count], *refs[count + len(after) :])

    moved = sum(a.size * a.dtype.itemsize for a in (*operands, *jax.tree.leaves(out_shape)))
    return pl.pallas_call(
        kernel,
        out_shape=out_shape,
        in_specs=[VMEM] * count + [ANY] * len(after),
        out_specs=jax.tree.map(lambda _: VMEM, out_shape),
        compiler_params=PARAMS,
        cost_estimate=pl.CostEstimate(flops=flops, bytes_accessed=moved, transcendentals=0),
    )(*operands, *after)


def shape(dims, dtype):
    return jax.ShapeDtypeStruct(dims, dtype)


def row_sums(terms, tok):
    total = jnp.zeros((tok, 128), F32)
    for v in terms:
        for j in range(0, v.shape[1], 128):
            total = total + v[:, j : j + 128]
    return jnp.sum(total.T, axis=0, keepdims=True)


def as_column(row):
    return jnp.broadcast_to(row, (128, row.shape[1])).T[:, :1]


def partials_kernel(ny, far, ck, cv, wk, wv, *outs):
    half, y = lax.axis_index("tensor") // ny, lax.axis_index("tensor") % ny
    c = jnp.concatenate([ck[...], cv[...]], axis=1)
    for k in range(ny):
        out = outs[k] if far else outs[0].at[k]
        cols = out.shape[1]
        owner = (1 - half) * ny + (y + k) % ny if far else half * ny + k
        at = pl.ds(pl.multiple_of(owner * cols, cols), cols)
        w = jnp.concatenate([wk[0, at, :], wv[0, at, :]], axis=1)
        out[...] = lax.dot_general(c, w, (((1,), (1,)), ((), ())), preferred_element_type=F32).astype(BF16)


def pieces(row):
    high = row.astype(BF16)
    rest = row - high.astype(F32)
    mid = rest.astype(BF16)
    return high, mid, (rest - mid.astype(F32)).astype(BF16)


def send_kernel(ny, other, near, near_parts, *refs):
    parts, (send, centre) = refs[:ny], refs[ny:]
    tok, cols = parts[0].shape
    total = sum(p[...].astype(F32) for p in parts).astype(BF16)
    send[:tok] = total
    send[tok:] = jnp.zeros((PAD, cols), BF16)

    def weighted(grad, block):
        return grad.astype(F32) * block[tok : tok + 1].astype(F32) * block[:tok].astype(F32)

    terms = [weighted(total, other)] + [weighted(near_parts[i], near.at[i]) for i in range(ny)]
    row = row_sums(terms, tok)
    centre[...] = row
    for i, piece in enumerate(pieces(row)):
        send[tok + i : tok + i + 1, :tok] = piece


def copy_kernel(a, out):
    out[...] = a[...]


def half_steps(lr, side, rs, blocks, owners, ck, cv, wk, wv, new):
    tok, width = ck.shape
    cols = blocks[0].shape[1]
    c = jnp.concatenate([ck[...], cv[...]], axis=1)
    for b, owner in zip(blocks, owners):
        here = pl.ds(pl.multiple_of(owner * cols, cols), cols)
        at = pl.ds(pl.multiple_of((side * len(blocks) + owner) * cols, cols), cols)
        normed = (b[:tok].astype(F32) * rs * b[tok : tok + 1].astype(F32)).astype(BF16)
        step = lax.dot_general(normed, c, (((0,), (0,)), ((), ())), preferred_element_type=F32)
        step = step.astype(BF16).astype(F32)
        new[0, here, :] = (wk[0, at, :].astype(F32) - lr * step[:, :width]).astype(BF16)
        new[1, here, :] = (wv[0, at, :].astype(F32) - lr * step[:, width:]).astype(BF16)


def near_kernel(ny, lr, features, near, *refs):
    far, weights, (new, rs_out) = refs[:ny], refs[ny:-2], refs[-2:]
    near = [near.at[i] for i in range(ny)]
    tok = far[0].shape[0] - PAD
    total = jnp.zeros((tok, 128), F32)
    for b in (*near, *far):
        v = b[:tok].astype(F32)
        v = v * v
        for j in range(0, v.shape[1], 128):
            total = total + v[:, j : j + 128]
    rs = lax.rsqrt(jnp.sum(total, axis=1, keepdims=True) / features + EPS)
    rs_out[...] = rs
    half_steps(lr, lax.axis_index("tensor") // ny, rs, near, range(ny), *weights, new)


def far_kernel(ny, lr, rs, *refs):
    far, weights, new = refs[:ny], refs[ny:-1], refs[-1]
    me = lax.axis_index("tensor")
    owners = [(me % ny + ny - k) % ny for k in range(ny)]
    half_steps(lr, 1 - me // ny, rs[...], far, owners, *weights, new)


def gain_kernel(near, far, x, gain, rs, new_gain):
    ng = near[...].astype(F32) + far[: near.shape[0]].astype(F32)
    step = jnp.sum(ng * x[...].astype(F32) * rs[...], axis=0, keepdims=True).astype(BF16).astype(F32)
    new_gain[...] = (gain[...].astype(F32) - LR_GAIN * step).astype(BF16)


def grad_kernel(features, near, far, x, gain, rs, *refs):
    centres, grad = refs[:-1], refs[-1]
    ng = near[...].astype(F32) + far[: near.shape[0]].astype(F32)
    xf = x[...].astype(F32)
    r = rs[...]
    mean = as_column(sum(c[...] for c in centres) / features)
    grad[...] = (r * gain[...].astype(F32) * ng - xf * (r * r * r * mean)).astype(BF16)


def average_pair(mine, theirs):
    return ((mine.astype(F32) + theirs.astype(F32)) * 0.5).astype(BF16)


def average_half(side, new, other, into, after=()):
    rows, width = new.shape[1:]
    tile = rows // 2
    first = isinstance(into[0], jax.ShapeDtypeStruct)
    extra = (*after,) if first else (*into, *after)

    def kernel(side_ref, a, b, *refs):
        for i, out in enumerate(refs[len(extra) :]):
            out[0] = average_pair(a[i], b[i])

    pair = pl.BlockSpec((2, tile, width), lambda i, s: (0, i, 0))
    whole = pl.BlockSpec((1, tile, width), lambda i, s: (0, s[0] * 2 + i, 0))
    return pl.pallas_call(
        kernel,
        out_shape=[shape(a.shape, a.dtype) for a in into],
        grid_spec=pltpu.PrefetchScalarGridSpec(
            num_scalar_prefetch=1,
            grid=(2,),
            in_specs=[pair, pair] + [ANY] * len(extra),
            out_specs=[whole, whole],
        ),
        input_output_aliases={} if first else {3: 0, 4: 1},
        compiler_params=PARAMS,
        cost_estimate=pl.CostEstimate(flops=4 * rows * width, bytes_accessed=12 * rows * width, transcendentals=0),
    )(side, new, other, *extra)


def step_at(offset, nt, nr, tokens, norm_gain, key_weight, value_weight, key_cotangent, value_cotangent):
    ny = nt // 2
    tok, cols = tokens.shape
    width = key_cotangent.shape[1]
    features = cols * nt
    lr = 0.25 / tok
    weights = (key_cotangent, value_cotangent, key_weight, value_weight)
    row = shape((1, tok), F32)

    def over_tensor(a, to):
        return lax.ppermute(a, "tensor", [(i, to(i)) for i in range(nt)])

    def over_z(a):
        return over_tensor(a, lambda i: (i + ny) % nt)

    def along_y(a, k):
        return over_tensor(a, lambda i: i // ny * ny + (i + k) % ny)

    def over_y(a):
        return [along_y(a, k) for k in range(1, ny)]

    def fetch(a):
        return lax.ppermute(a, "replica", [(i, (i - offset) % nr) for i in range(nr)])

    groups = [list(range(ny)), list(range(ny, nt))]

    def gather_y(a):
        return lax.all_gather(a, "tensor", axis_index_groups=groups)

    mine = jnp.concatenate([tokens, jnp.broadcast_to(norm_gain, (PAD, cols))], axis=0)
    other = over_z(mine)

    block, work = shape((tok, cols), BF16), 2 * tok * features * width
    far_parts = call(functools.partial(partials_kernel, ny, True), (block,) * ny, weights, work)
    near_parts = call(
        functools.partial(partials_kernel, ny, False),
        shape((ny, tok, cols), BF16),
        weights,
        work,
        after=(far_parts[0], mine),
    )
    near_sum = lax.psum_scatter(near_parts, "tensor", scatter_dimension=0, axis_index_groups=groups)
    far_parts = [far_parts[0]] + [along_y(far_parts[k], k) for k in range(1, ny)]

    near_blocks = gather_y(mine)
    send, centre = call(
        functools.partial(send_kernel, ny),
        (shape((tok + PAD, cols), BF16), shape((1, tok), F32)),
        (other, near_blocks, near_parts, *far_parts),
        6 * ny * tok * cols,
    )
    recv = over_z(send)
    again = call(copy_kernel, shape(other.shape, BF16), (other,), 0, after=(send,))
    far_blocks = (other, *over_y(again))

    half = shape((2, ny * cols, width), BF16)
    new_near, rs = call(
        functools.partial(near_kernel, ny, lr, features),
        (half, shape((tok, 1), F32)),
        (near_blocks, *far_blocks, *weights),
        2 * tok * features * width,
    )
    other_near = fetch(new_near)
    new_far = call(
        functools.partial(far_kernel, ny, lr),
        half,
        (rs, *far_blocks, *weights),
        2 * tok * features * width,
        after=(recv,),
    )
    other_far = fetch(new_far)

    centre = centre + jnp.sum(recv[tok : tok + 3, :tok].astype(F32), axis=0, keepdims=True)
    centres = (centre, *over_y(centre))

    new_gain = call(gain_kernel, shape((1, cols), BF16), (near_sum, recv, tokens, norm_gain, rs), 4 * tok * cols)
    other_gain = fetch(new_gain)
    input_grad = call(
        functools.partial(grad_kernel, features),
        shape((tok, cols), BF16),
        (near_sum, recv, tokens, norm_gain, rs, *centres),
        8 * tok * cols,
    )

    z = (lax.axis_index("tensor") // ny).astype(jnp.int32)[None]
    mixed = [shape(key_weight.shape, BF16)] * 2
    mixed = average_half(z, new_near, other_near, mixed, after=(input_grad,))
    mixed_key, mixed_value = average_half(1 - z, new_far, other_far, mixed)
    return mixed_key, mixed_value, new_gain, other_gain, input_grad


def per_device(*args):
    nt, nr = lax.axis_size("tensor"), lax.axis_size("replica")
    levels = nr.bit_length() - 1
    level = jnp.mod(args[-1][0], levels)
    branches = [functools.partial(step_at, 2**j, nt, nr) for j in range(levels)]
    mixed_key, mixed_value, new_gain, other_gain, input_grad = lax.switch(level, branches, *args[:-1])
    return mixed_key, mixed_value, average_pair(new_gain, other_gain), input_grad


def solution(mesh):
    rows, weights = P("replica", "tensor"), P("replica", None, "tensor")
    return jax.shard_map(
        per_device,
        mesh=mesh,
        in_specs=(rows, rows, weights, weights, rows, rows, P()),
        out_specs=(weights, weights, rows, rows),
        check_vma=False,
    )
```

time: 176 us -> 160 us (0.909)
  waiting for transfers between devices: 75.9 us -> 47.4 us
  starting transfers between devices: 66.8 us -> 76.6 us
  Pallas kernels: 10.9 us -> 13.9 us
    ppermute x11, waiting for transfers between devices: 75 us -> 29.7 us  [over_tensor(): return lax.ppermute(a, 'tensor', [(i, to(i)) for i in range(nt)])]
    ppermute x3, waiting for transfers between devices: 0.83 us -> 17.7 us  [fetch(): lax.ppermute(a, 'replica', [(i, (i - offset) % nr) for i in range(nr)])]
    ppermute x3, starting transfers between devices: 13.9 us -> 25 us  [fetch(): lax.ppermute(a, 'replica', [(i, (i - offset) % nr) for i in range(nr)])]
    convert_element_type x3 -> x1, other arithmetic: 4.43 us -> 1.27 us  [average_pair(): return ((mine.astype(F32) + theirs.astype(F32)) * 0.5).astype(BF16)]
    pallas_call x4 -> x10, Pallas kernels: 10.9 us -> 13.9 us  [the longest x8 10.2 us: call(): pl.pallas_call(kernel, out_shape=out_shape, in_specs=[VMEM] * count + [AN...]
  transfers between devices with their start and end apart: 16 -> 16, of which waited for: 9 -> 6; matrix products, arithmetic and copies ran while one was open for 3% -> 0% of each run, Pallas kernels for 4% -> 9%
where the time goes in v2:
time: 160 us; the launch traced here: 159 us
  starting transfers between devices  76.6 us (48%)
  waiting for transfers between devices  47.4 us (30%)
  between operations  14.7 us (9%)
  Pallas kernels  13.9 us (9%)
  other arithmetic  3.68 us (2%)
  local copies, waits for them, and re-layouts  2.26 us (1%)
    ppermute x11, starting transfers between devices, over_tensor(): return lax.ppermute(a, 'tensor', [(i, to(i)) for i in range(nt)])  51.5 us
    ppermute x11, waiting for transfers between devices, over_tensor(): return lax.ppermute(a, 'tensor', [(i, to(i)) for i in range(nt)])  29.7 us
    ppermute x3, starting transfers between devices, fetch(): lax.ppermute(a, 'replica', [(i, (i - offset) % nr) for i in range(nr)])  25 us
    ppermute x3, waiting for transfers between devices, fetch(): lax.ppermute(a, 'replica', [(i, (i - offset) % nr) for i in range(nr)])  17.7 us
    pallas_call x8, Pallas kernels, call(): pl.pallas_call(kernel, out_shape=out_shape, in_specs=[VMEM] * count + [AN...  10.2 us
    pallas_call x2, Pallas kernels, average_half(): pl.pallas_call(kernel, out_shape=[shape(a.shape, a.dtype) for a in into],...  3.63 us
  transfers between devices with their start and end apart: 16, of which 6 were waited for; matrix products, arithmetic and copies ran while one was open for 0% of the time, Pallas kernels for 9%

profile of v2, /device:TPU:1, one launch (start us, length us, event | category | flops | bytes accessed | tf_op | source)
XLA Modules:
  0.0 159.1 jit_solution(1371813567105856557)
XLA Ops:
  7.8 143.2 %conditional.4 = (bf16[1,4096,128]{2,1,0:T(8,128)(2,1)}, bf16[1,4096,128]{2,1,0:T(8,128)(2,1)}, bf16[1,512]{1,0:T(2,128)(2,1)}, bf16[256,512]{1,0:T(8,128)(2,1)}, bf16[1,512]{1,0:T(2,128)(2,1)}) conditional(s32[]{:T(128)} %clamp.3, (bf16[1,512]{1,0:T(2,128)(2,1)}, bf16[256,512]{1,0:T(8,128)(2,1)}, ...), branch_computations={%region_0.3_spmd, %region_3.6_spmd, %region_6.9_spmd, %region_9.12... | conditional | flops 1081116160 | bytes 85501672
  8.1 0.0 all-gather.19.cloned.1.call-start
  8.1 0.7 reduce.3
  8.8 1.7 %pad_maximum_fusion.3.refs_5_ = bf16[272,512]{1,0:T(8,128)(2,1)} fusion(bf16[16,512]{1,0:T(8,128)(2,1)S(1)} %broadcast_in_dim.68, bf16[256,512]{1,0:T(8,128)(2,1)} %get-tuple-element.140.refs_2_), kind=kLoop, calls=%fused_computation.6 | loop fusion | flops 557056 | bytes 557056 | tf_op jit(solution)/shard_map/cond/branch_3_fun/concatenate | solution.py:204
  10.5 0.0 all-gather.19.cloned.1.call-update
  10.5 0.0 reduce-scatter.13.cloned.1.call-start
  10.6 0.0 copy-start.15
  10.6 0.0 copy-start.36
  10.6 0.0 copy-start.63
  10.6 0.0 copy-start.72
  10.6 2.2 %branch_3_fun.10 = (bf16[256,512]{1,0:T(8,128)(2,1)S(1)}, bf16[256,512]{1,0:T(8,128)(2,1)S(1)}, bf16[256,512]{1,0:T(8,128)(2,1)S(1)}, bf16[256,512]{1,0:T(8,128)(2,1)S(1)}) custom-call(bf16[256,128]{1,0:T(8,128)(2,1)} %get-tuple-element.142.refs_0_.refs_5_, bf16[256,128]{1,0:T(8,128)(2,1)} %get-tuple-element.143.refs_1_.refs_6_, ...), custom_call_target="tpu_custom_call" | custom-call | flops 268435456 | bytes 3276800 | tf_op jit(solution)/shard_map/cond/branch_3_fun/pallas_call | solution.py:27
  12.9 0.0 copy-done.48
  12.9 0.0 copy-done.15
  12.9 0.0 copy-done.36
  12.9 0.0 copy-done.63
  12.9 0.0 copy-done.72
  12.9 1.5 branch_3_fun.11.refs_2_
  14.4 0.0 reduce-scatter.13.cloned.1.call-update
  14.4 16.3 %collective-permute-start.42 = (bf16[272,512]{1,0:T(8,128)(2,1)S(1)}, bf16[272,512]{1,0:T(8,128)(2,1)S(1)}, u32[]{:S(2)}, u32[]{:S(2)}) collective-permute-start(bf16[272,512]{1,0:T(8,128)(2,1)S(1)} %copy-done.15), channel_id=1, source_target_pairs={{0,4},{1,5},{2,6},{3,7},{4,0},{5,1},{6,2},{7,3},{8,12},{9,13},{10,... | collective-permute-start | bytes 835592 | tf_op jit(solution)/shard_map/cond/branch_3_fun/ppermute | solution.py:185
  30.7 3.2 %collective-permute-start.43 = (bf16[256,512]{1,0:T(8,128)(2,1)S(1)}, bf16[256,512]{1,0:T(8,128)(2,1)S(1)}, u32[]{:S(2)}, u32[]{:S(2)}) collective-permute-start(bf16[256,512]{1,0:T(8,128)(2,1)S(1)} %get-tuple-element.147), channel_id=1, source_target_pairs={{0,1},{1,2},{2,3},{3,0},{4,5},{5,6},{6,7},{7,4},{8,9},{9,10},{10,1... | collective-permute-start | bytes 786440 | tf_op jit(solution)/shard_map/cond/branch_3_fun/ppermute | solution.py:185
  33.9 4.5 %collective-permute-start.44 = (bf16[256,512]{1,0:T(8,128)(2,1)S(1)}, bf16[256,512]{1,0:T(8,128)(2,1)S(1)}, u32[]{:S(2)}, u32[]{:S(2)}) collective-permute-start(bf16[256,512]{1,0:T(8,128)(2,1)S(1)} %get-tuple-element.148), channel_id=1, source_target_pairs={{0,2},{1,3},{2,0},{3,1},{4,6},{5,7},{6,4},{7,5},{8,10},{9,11},{10,... | collective-permute-start | bytes 786440 | tf_op jit(solution)/shard_map/cond/branch_3_fun/ppermute | solution.py:185
  38.4 3.0 %collective-permute-start.45 = (bf16[256,512]{1,0:T(8,128)(2,1)S(1)}, bf16[256,512]{1,0:T(8,128)(2,1)S(1)}, u32[]{:S(2)}, u32[]{:S(2)}) collective-permute-start(bf16[256,512]{1,0:T(8,128)(2,1)S(1)} %get-tuple-element.149), channel_id=1, source_target_pairs={{0,3},{1,0},{2,1},{3,2},{4,7},{5,4},{6,5},{7,6},{8,11},{9,8},{10,9... | collective-permute-start | bytes 786440 | tf_op jit(solution)/shard_map/cond/branch_3_fun/ppermute | solution.py:185
  41.4 1.7 %collective-permute-done.43.refs_4_ = bf16[256,512]{1,0:T(8,128)(2,1)S(1)} collective-permute-done((bf16[256,512]{1,0:T(8,128)(2,1)S(1)}, bf16[256,512]{1,0:T(8,128)(2,1)S(1)}, u32[]{:S(2)}, u32[]{:S(2)}) %collective-permute-start.43) | collective-permute-done | bytes 262176 | tf_op jit(solution)/shard_map/cond/branch_3_fun/ppermute | solution.py:185
  43.2 13.7 %collective-permute-done.44.refs_5_ = bf16[256,512]{1,0:T(8,128)(2,1)S(1)} collective-permute-done((bf16[256,512]{1,0:T(8,128)(2,1)S(1)}, bf16[256,512]{1,0:T(8,128)(2,1)S(1)}, u32[]{:S(2)}, u32[]{:S(2)}) %collective-permute-start.44) | collective-permute-done | bytes 262176 | tf_op jit(solution)/shard_map/cond/branch_3_fun/ppermute | solution.py:185
  56.9 0.2 collective-permute-done.45.refs_6_
  57.1 0.0 collective-permute-done.42.refs_0_.refs_1_
  57.1 1.2 copy-done.6
  58.4 2.0 %branch_3_fun.12 = (bf16[272,512]{1,0:T(8,128)(2,1)S(1)}, f32[1,256]{1,0:T(1,128)S(1)}) custom-call(bf16[272,512]{1,0:T(8,128)(2,1)S(1)} %collective-permute-done.42.refs_0_.refs_1_, bf16[4,272,512]{2,1,0:T(8,128)(2,1)S(1)} %bitcast.31, bf16[4,256,512]{2,1,0:T(8,128)(2,1)} %branch_3_fun.11.refs_2_, bf16[256,512]{1,0:T(8,128)(2,1)S(1)} %get-tuple-element.146.refs_4_.refs_3_, ...), custom_call_target="tpu_custom_call" | custom-call | flops 3145728 | bytes 3769344 | tf_op jit(solution)/shard_map/cond/branch_3_fun/pallas_call | solution.py:27
  60.4 5.1 %collective-permute-start.48 = (bf16[272,512]{1,0:T(8,128)(2,1)S(1)}, bf16[272,512]{1,0:T(8,128)(2,1)S(1)}, u32[]{:S(2)}, u32[]{:S(2)}) collective-permute-start(bf16[272,512]{1,0:T(8,128)(2,1)S(1)} %branch_3_fun.13), channel_id=1, source_target_pairs={{0,3},{1,0},{2,1},{3,2},{4,7},{5,4},{6,5},{7,6},{8,11},{9,8},{10,9... | collective-permute-start | bytes 835592 | tf_op jit(solution)/shard_map/cond/branch_3_fun/ppermute | solution.py:185
  65.5 1.9 %collective-permute-start.47 = (bf16[272,512]{1,0:T(8,128)(2,1)S(1)}, bf16[272,512]{1,0:T(8,128)(2,1)S(1)}, u32[]{:S(2)}, u32[]{:S(2)}) collective-permute-start(bf16[272,512]{1,0:T(8,128)(2,1)S(1)} %branch_3_fun.13), channel_id=1, source_target_pairs={{0,2},{1,3},{2,0},{3,1},{4,6},{5,7},{6,4},{7,5},{8,10},{9,11},{10,... | collective-permute-start | bytes 835592 | tf_op jit(solution)/shard_map/cond/branch_3_fun/ppermute | solution.py:185
  67.4 2.5 %collective-permute-start.46 = (bf16[272,512]{1,0:T(8,128)(2,1)S(1)}, bf16[272,512]{1,0:T(8,128)(2,1)S(1)}, u32[]{:S(2)}, u32[]{:S(2)}) collective-permute-start(bf16[272,512]{1,0:T(8,128)(2,1)S(1)} %branch_3_fun.13), channel_id=1, source_target_pairs={{0,1},{1,2},{2,3},{3,0},{4,5},{5,6},{6,7},{7,4},{8,9},{9,10},{10,1... | collective-permute-start | bytes 835592 | tf_op jit(solution)/shard_map/cond/branch_3_fun/ppermute | solution.py:185
  69.9 5.1 %collective-permute-start.49 = (bf16[272,512]{1,0:T(8,128)(2,1)S(1)}, bf16[272,512]{1,0:T(8,128)(2,1)S(1)}, u32[]{:S(2)}, u32[]{:S(2)}) collective-permute-start(bf16[272,512]{1,0:T(8,128)(2,1)S(1)} %get-tuple-element.150.refs_1_), channel_id=1, source_target_pairs={{0,4},{1,5},{2,6},{3,7},{4,0},{5,1},{6,2},{7,3},{8,12},{9,13},{10,... | collective-permute-start | bytes 835592 | tf_op jit(solution)/shard_map/cond/branch_3_fun/ppermute | solution.py:185
  75.0 1.8 %collective-permute-done.48.refs_4_ = bf16[272,512]{1,0:T(8,128)(2,1)S(1)} collective-permute-done((bf16[272,512]{1,0:T(8,128)(2,1)S(1)}, bf16[272,512]{1,0:T(8,128)(2,1)S(1)}, u32[]{:S(2)}, u32[]{:S(2)}) %collective-permute-start.48) | collective-permute-done | bytes 278560 | tf_op jit(solution)/shard_map/cond/branch_3_fun/ppermute | solution.py:185
  76.7 0.0 collective-permute-done.47.refs_3_
  76.7 12.3 %collective-permute-done.46.refs_2_ = bf16[272,512]{1,0:T(8,128)(2,1)S(1)} collective-permute-done((bf16[272,512]{1,0:T(8,128)(2,1)S(1)}, bf16[272,512]{1,0:T(8,128)(2,1)S(1)}, u32[]{:S(2)}, u32[]{:S(2)}) %collective-permute-start.46) | collective-permute-done | bytes 278560 | tf_op jit(solution)/shard_map/cond/branch_3_fun/ppermute | solution.py:185
  89.0 0.0 copy-done.7
  89.0 0.0 copy-done.37
  89.0 0.0 copy-done.49
  89.0 0.0 copy-done.73
  89.0 2.1 %branch_3_fun.14 = (bf16[2,2048,128]{2,1,0:T(8,128)(2,1)}, f32[256,1]{1,0:T(8,128)S(1)}) custom-call(bf16[4,272,512]{2,1,0:T(8,128)(2,1)S(1)} %bitcast.32, bf16[272,512]{1,0:T(8,128)(2,1)S(1)} %collective-permute-done.42.refs_0_.refs_1_, bf16[272,512]{1,0:T(8,128)(2,1)S(1)} %collective-permute-done.46.refs_2_, ...), custom_call_target="tpu_custom_call" | custom-call | flops 268435456 | bytes 5506048 | tf_op jit(solution)/shard_map/cond/branch_3_fun/pallas_call | solution.py:27
  91.1 4.5 %collective-permute-start.51 = (bf16[2,2048,128]{2,1,0:T(8,128)(2,1)}, bf16[2,2048,128]{2,1,0:T(8,128)(2,1)}, u32[]{:S(2)}, u32[]{:S(2)}) collective-permute-start(bf16[2,2048,128]{2,1,0:T(8,128)(2,1)} %get-tuple-element.152.a), channel_id=1, source_target_pairs={{0,448},{8,456},{16,464},{24,472},{32,480},{40,488},{48,496},{56,5... | collective-permute-start | bytes 3145736 | tf_op jit(solution)/shard_map/cond/branch_3_fun/ppermute | solution.py:197
  95.7 0.0 collective-permute-done.49.refs_9_.refs_1_
  95.7 0.0 copy-start.57
  95.7 0.0 copy-start.81
  95.7 0.7 branch_3_fun.15.a
  96.4 16.6 %collective-permute-start.50 = (bf16[2,2048,128]{2,1,0:T(8,128)(2,1)S(1)}, bf16[2,2048,128]{2,1,0:T(8,128)(2,1)S(1)}, u32[]{:S(2)}, u32[]{:S(2)}) collective-permute-start(bf16[2,2048,128]{2,1,0:T(8,128)(2,1)S(1)} %branch_3_fun.15.a), channel_id=1, source_target_pairs={{0,448},{8,456},{16,464},{24,472},{32,480},{40,488},{48,496},{56,5... | collective-permute-start | bytes 3145736 | tf_op jit(solution)/shard_map/cond/branch_3_fun/ppermute | solution.py:197
  113.0 4.6 %collective-permute-start.54 = (f32[1,256]{1,0:T(1,128)S(1)}, f32[1,256]{1,0:T(1,128)S(1)}, u32[]{:S(2)}, u32[]{:S(2)}) collective-permute-start(f32[1,256]{1,0:T(1,128)S(1)} %add.38.refs_5_), channel_id=1, source_target_pairs={{0,3},{1,0},{2,1},{3,2},{4,7},{5,4},{6,5},{7,6},{8,11},{9,8},{10,9... | collective-permute-start | bytes 3080 | tf_op jit(solution)/shard_map/cond/branch_3_fun/ppermute | solution.py:185
  117.6 2.7 %collective-permute-start.53 = (f32[1,256]{1,0:T(1,128)S(1)}, f32[1,256]{1,0:T(1,128)S(1)}, u32[]{:S(2)}, u32[]{:S(2)}) collective-permute-start(f32[1,256]{1,0:T(1,128)S(1)} %add.38.refs_5_), channel_id=1, source_target_pairs={{0,2},{1,3},{2,0},{3,1},{4,6},{5,7},{6,4},{7,5},{8,10},{9,11},{10,... | collective-permute-start | bytes 3080 | tf_op jit(solution)/shard_map/cond/branch_3_fun/ppermute | solution.py:185
  120.3 2.8 %collective-permute-start.52 = (f32[1,256]{1,0:T(1,128)S(1)}, f32[1,256]{1,0:T(1,128)S(1)}, u32[]{:S(2)}, u32[]{:S(2)}) collective-permute-start(f32[1,256]{1,0:T(1,128)S(1)} %add.38.refs_5_), channel_id=1, source_target_pairs={{0,1},{1,2},{2,3},{3,0},{4,5},{5,6},{6,7},{7,4},{8,9},{9,10},{10,1... | collective-permute-start | bytes 3080 | tf_op jit(solution)/shard_map/cond/branch_3_fun/ppermute | solution.py:185
  123.1 0.0 reduce-scatter.13.cloned.1.call-done
  123.1 0.0 copy-done.57
  123.2 0.9 copy-done.24
  124.1 0.7 branch_3_fun.19
  124.8 0.0 collective-permute-done.54.refs_8_
  124.8 3.9 %collective-permute-start.55 = (bf16[1,512]{1,0:T(2,128)(2,1)}, bf16[1,512]{1,0:T(2,128)(2,1)}, u32[]{:S(2)}, u32[]{:S(2)}) collective-permute-start(bf16[1,512]{1,0:T(2,128)(2,1)} %branch_3_fun.19), channel_id=1, source_target_pairs={{0,448},{8,456},{16,464},{24,472},{32,480},{40,488},{48,496},{56,5... | collective-permute-start | bytes 3080 | tf_op jit(solution)/shard_map/cond/branch_3_fun/ppermute | solution.py:197
  128.8 0.0 collective-permute-done.53.refs_7_
  128.8 0.0 collective-permute-done.52.refs_6_
  128.8 0.9 branch_3_fun.16.refs_0_
  129.7 0.0 collective-permute-done.51.b
  129.7 2.4 %branch_3_fun.17 = (bf16[1,4096,128]{2,1,0:T(8,128)(2,1)}, bf16[1,4096,128]{2,1,0:T(8,128)(2,1)}) custom-call(s32[1]{0:T(128)} %bitcast.12.side_ref, bf16[2,2048,128]{2,1,0:T(8,128)(2,1)} %get-tuple-element.152.a, bf16[2,2048,128]{2,1,0:T(8,128)(2,1)} %collective-permute-done.51.b, bf16[256,512]{1,0:T(8,128)(2,1)} %branch_3_fun.16.refs_0_), custom_call_target="tpu_custom_call" | custom-call | flops 1048576 | bytes 3145728 | tf_op jit(solution)/shard_map/cond/branch_3_fun/pallas_call | solution.py:160
  132.1 17.7 %collective-permute-done.50.b = bf16[2,2048,128]{2,1,0:T(8,128)(2,1)S(1)} collective-permute-done((bf16[2,2048,128]{2,1,0:T(8,128)(2,1)S(1)}, bf16[2,2048,128]{2,1,0:T(8,128)(2,1)S(1)}, u32[]{:S(2)}, u32[]{:S(2)}) %collective-permute-start.50) | collective-permute-done | bytes 1048608 | tf_op jit(solution)/shard_map/cond/branch_3_fun/ppermute | solution.py:197
  149.8 1.2 branch_3_fun.18
  151.0 0.0 collective-permute-done.55
  151.0 1.3 fusion.1
  (15 shorter events, 0.1 us)
Async XLA Ops:
  8.1 49.0 %all-gather.19.cloned.1.call-start = ((), (), s32[]{:S(2)}) async-start(), calls=%async_computation.13 | async-start | bytes 1392640 | tf_op jit(solution)/shard_map/cond/branch_3_fun/all_gather | solution.py:202
  10.5 2.4 %copy-start.48 = (bf16[1,4096,128]{2,1,0:T(8,128)(2,1)S(1)}, bf16[1,4096,128]{2,1,0:T(8,128)(2,1)}, u32[]{:S(2)}) copy-start(bf16[1,4096,128]{2,1,0:T(8,128)(2,1)} %get-tuple-element.145.refs_3_.refs_8_) | copy-start | bytes 3145732
  10.5 112.6 %reduce-scatter.13.cloned.1.call-start = ((), (), s32[]{:S(2)}) async-start(), calls=%async_computation.12 | async-start | bytes 1310720 | tf_op jit(solution)/shard_map/cond/branch_3_fun/reduce_scatter | solution.py:216
  10.6 2.3 %copy-start.15 = (bf16[272,512]{1,0:T(8,128)(2,1)S(1)}, bf16[272,512]{1,0:T(8,128)(2,1)}, u32[]{:S(2)}) copy-start(bf16[272,512]{1,0:T(8,128)(2,1)} %pad_maximum_fusion.3.refs_5_) | copy-start | bytes 835588
  10.6 2.3 %copy-start.36 = (bf16[1,4096,128]{2,1,0:T(8,128)(2,1)S(1)}, bf16[1,4096,128]{2,1,0:T(8,128)(2,1)}, u32[]{:S(2)}) copy-start(bf16[1,4096,128]{2,1,0:T(8,128)(2,1)} %get-tuple-element.144.refs_2_.refs_7_) | copy-start | bytes 3145732
  10.6 2.3 %copy-start.63 = (bf16[256,128]{1,0:T(8,128)(2,1)S(1)}, bf16[256,128]{1,0:T(8,128)(2,1)}, u32[]{:S(2)}) copy-start(bf16[256,128]{1,0:T(8,128)(2,1)} %get-tuple-element.142.refs_0_.refs_5_) | copy-start | bytes 196612
  10.6 2.3 %copy-start.72 = (bf16[256,128]{1,0:T(8,128)(2,1)S(1)}, bf16[256,128]{1,0:T(8,128)(2,1)}, u32[]{:S(2)}) copy-start(bf16[256,128]{1,0:T(8,128)(2,1)} %get-tuple-element.143.refs_1_.refs_6_) | copy-start | bytes 196612
  14.4 42.7 %collective-permute-start.42 = (bf16[272,512]{1,0:T(8,128)(2,1)S(1)}, bf16[272,512]{1,0:T(8,128)(2,1)S(1)}, u32[]{:S(2)}, u32[]{:S(2)}) collective-permute-start(bf16[272,512]{1,0:T(8,128)(2,1)S(1)} %copy-done.15), channel_id=1, source_target_pairs={{0,4},{1,5},{2,6},{3,7},{4,0},{5,1},{6,2},{7,3},{8,12},{9,13},{10,... | collective-permute-start | bytes 835592 | tf_op jit(solution)/shard_map/cond/branch_3_fun/ppermute | solution.py:185
  30.7 12.5 %collective-permute-start.43 = (bf16[256,512]{1,0:T(8,128)(2,1)S(1)}, bf16[256,512]{1,0:T(8,128)(2,1)S(1)}, u32[]{:S(2)}, u32[]{:S(2)}) collective-permute-start(bf16[256,512]{1,0:T(8,128)(2,1)S(1)} %get-tuple-element.147), channel_id=1, source_target_pairs={{0,1},{1,2},{2,3},{3,0},{4,5},{5,6},{6,7},{7,4},{8,9},{9,10},{10,1... | collective-permute-start | bytes 786440 | tf_op jit(solution)/shard_map/cond/branch_3_fun/ppermute | solution.py:185
  33.9 23.0 %collective-permute-start.44 = (bf16[256,512]{1,0:T(8,128)(2,1)S(1)}, bf16[256,512]{1,0:T(8,128)(2,1)S(1)}, u32[]{:S(2)}, u32[]{:S(2)}) collective-permute-start(bf16[256,512]{1,0:T(8,128)(2,1)S(1)} %get-tuple-element.148), channel_id=1, source_target_pairs={{0,2},{1,3},{2,0},{3,1},{4,6},{5,7},{6,4},{7,5},{8,10},{9,11},{10,... | collective-permute-start | bytes 786440 | tf_op jit(solution)/shard_map/cond/branch_3_fun/ppermute | solution.py:185
  38.4 18.7 %collective-permute-start.45 = (bf16[256,512]{1,0:T(8,128)(2,1)S(1)}, bf16[256,512]{1,0:T(8,128)(2,1)S(1)}, u32[]{:S(2)}, u32[]{:S(2)}) collective-permute-start(bf16[256,512]{1,0:T(8,128)(2,1)S(1)} %get-tuple-element.149), channel_id=1, source_target_pairs={{0,3},{1,0},{2,1},{3,2},{4,7},{5,4},{6,5},{7,6},{8,11},{9,8},{10,9... | collective-permute-start | bytes 786440 | tf_op jit(solution)/shard_map/cond/branch_3_fun/ppermute | solution.py:185
  57.1 1.2 copy-start.6
  58.4 30.6 %copy-start.7 = (bf16[1088,512]{1,0:T(8,128)(2,1)S(1)}, bf16[1088,512]{1,0:T(8,128)(2,1)}, u32[]{:S(2)}) copy-start(bf16[1088,512]{1,0:T(8,128)(2,1)} %all-gather.19.cloned.1.call-done) | copy-start | bytes 3342340
  58.4 30.6 %copy-start.37 = (bf16[1,4096,128]{2,1,0:T(8,128)(2,1)S(1)}, bf16[1,4096,128]{2,1,0:T(8,128)(2,1)}, u32[]{:S(2)}) copy-start(bf16[1,4096,128]{2,1,0:T(8,128)(2,1)} %get-tuple-element.144.refs_2_.refs_7_) | copy-start | bytes 3145732
  58.4 30.6 %copy-start.49 = (bf16[1,4096,128]{2,1,0:T(8,128)(2,1)S(1)}, bf16[1,4096,128]{2,1,0:T(8,128)(2,1)}, u32[]{:S(2)}) copy-start(bf16[1,4096,128]{2,1,0:T(8,128)(2,1)} %get-tuple-element.145.refs_3_.refs_8_) | copy-start | bytes 3145732
  58.4 30.6 %copy-start.73 = (bf16[256,128]{1,0:T(8,128)(2,1)S(1)}, bf16[256,128]{1,0:T(8,128)(2,1)}, u32[]{:S(2)}) copy-start(bf16[256,128]{1,0:T(8,128)(2,1)} %get-tuple-element.143.refs_1_.refs_6_) | copy-start | bytes 196612
  60.4 16.3 %collective-permute-start.48 = (bf16[272,512]{1,0:T(8,128)(2,1)S(1)}, bf16[272,512]{1,0:T(8,128)(2,1)S(1)}, u32[]{:S(2)}, u32[]{:S(2)}) collective-permute-start(bf16[272,512]{1,0:T(8,128)(2,1)S(1)} %branch_3_fun.13), channel_id=1, source_target_pairs={{0,3},{1,0},{2,1},{3,2},{4,7},{5,4},{6,5},{7,6},{8,11},{9,8},{10,9... | collective-permute-start | bytes 835592 | tf_op jit(solution)/shard_map/cond/branch_3_fun/ppermute | solution.py:185
  65.5 11.3 %collective-permute-start.47 = (bf16[272,512]{1,0:T(8,128)(2,1)S(1)}, bf16[272,512]{1,0:T(8,128)(2,1)S(1)}, u32[]{:S(2)}, u32[]{:S(2)}) collective-permute-start(bf16[272,512]{1,0:T(8,128)(2,1)S(1)} %branch_3_fun.13), channel_id=1, source_target_pairs={{0,2},{1,3},{2,0},{3,1},{4,6},{5,7},{6,4},{7,5},{8,10},{9,11},{10,... | collective-permute-start | bytes 835592 | tf_op jit(solution)/shard_map/cond/branch_3_fun/ppermute | solution.py:185
  67.4 21.6 %collective-permute-start.46 = (bf16[272,512]{1,0:T(8,128)(2,1)S(1)}, bf16[272,512]{1,0:T(8,128)(2,1)S(1)}, u32[]{:S(2)}, u32[]{:S(2)}) collective-permute-start(bf16[272,512]{1,0:T(8,128)(2,1)S(1)} %branch_3_fun.13), channel_id=1, source_target_pairs={{0,1},{1,2},{2,3},{3,0},{4,5},{5,6},{6,7},{7,4},{8,9},{9,10},{10,1... | collective-permute-start | bytes 835592 | tf_op jit(solution)/shard_map/cond/branch_3_fun/ppermute | solution.py:185
  69.9 25.8 %collective-permute-start.49 = (bf16[272,512]{1,0:T(8,128)(2,1)S(1)}, bf16[272,512]{1,0:T(8,128)(2,1)S(1)}, u32[]{:S(2)}, u32[]{:S(2)}) collective-permute-start(bf16[272,512]{1,0:T(8,128)(2,1)S(1)} %get-tuple-element.150.refs_1_), channel_id=1, source_target_pairs={{0,4},{1,5},{2,6},{3,7},{4,0},{5,1},{6,2},{7,3},{8,12},{9,13},{10,... | collective-permute-start | bytes 835592 | tf_op jit(solution)/shard_map/cond/branch_3_fun/ppermute | solution.py:185
  91.1 38.6 %collective-permute-start.51 = (bf16[2,2048,128]{2,1,0:T(8,128)(2,1)}, bf16[2,2048,128]{2,1,0:T(8,128)(2,1)}, u32[]{:S(2)}, u32[]{:S(2)}) collective-permute-start(bf16[2,2048,128]{2,1,0:T(8,128)(2,1)} %get-tuple-element.152.a), channel_id=1, source_target_pairs={{0,448},{8,456},{16,464},{24,472},{32,480},{40,488},{48,496},{56,5... | collective-permute-start | bytes 3145736 | tf_op jit(solution)/shard_map/cond/branch_3_fun/ppermute | solution.py:197
  95.7 27.4 %copy-start.57 = (bf16[256,512]{1,0:T(8,128)(2,1)S(1)}, bf16[256,512]{1,0:T(8,128)(2,1)}, u32[]{:S(2)}) copy-start(bf16[256,512]{1,0:T(8,128)(2,1)} %get-tuple-element.140.refs_2_) | copy-start | bytes 786436
  95.7 27.4 %copy-start.81 = (bf16[1,512]{1,0:T(2,128)(2,1)S(1)}, bf16[1,512]{1,0:T(2,128)(2,1)}, u32[]{:S(2)}) copy-start(bf16[1,512]{1,0:T(2,128)(2,1)} %get-tuple-element.141.refs_3_) | copy-start | bytes 3076
  96.4 53.4 %collective-permute-start.50 = (bf16[2,2048,128]{2,1,0:T(8,128)(2,1)S(1)}, bf16[2,2048,128]{2,1,0:T(8,128)(2,1)S(1)}, u32[]{:S(2)}, u32[]{:S(2)}) collective-permute-start(bf16[2,2048,128]{2,1,0:T(8,128)(2,1)S(1)} %branch_3_fun.15.a), channel_id=1, source_target_pairs={{0,448},{8,456},{16,464},{24,472},{32,480},{40,488},{48,496},{56,5... | collective-permute-start | bytes 3145736 | tf_op jit(solution)/shard_map/cond/branch_3_fun/ppermute | solution.py:197
  113.0 11.8 %collective-permute-start.54 = (f32[1,256]{1,0:T(1,128)S(1)}, f32[1,256]{1,0:T(1,128)S(1)}, u32[]{:S(2)}, u32[]{:S(2)}) collective-permute-start(f32[1,256]{1,0:T(1,128)S(1)} %add.38.refs_5_), channel_id=1, source_target_pairs={{0,3},{1,0},{2,1},{3,2},{4,7},{5,4},{6,5},{7,6},{8,11},{9,8},{10,9... | collective-permute-start | bytes 3080 | tf_op jit(solution)/shard_map/cond/branch_3_fun/ppermute | solution.py:185
  117.6 11.1 %collective-permute-start.53 = (f32[1,256]{1,0:T(1,128)S(1)}, f32[1,256]{1,0:T(1,128)S(1)}, u32[]{:S(2)}, u32[]{:S(2)}) collective-permute-start(f32[1,256]{1,0:T(1,128)S(1)} %add.38.refs_5_), channel_id=1, source_target_pairs={{0,2},{1,3},{2,0},{3,1},{4,6},{5,7},{6,4},{7,5},{8,10},{9,11},{10,... | collective-permute-start | bytes 3080 | tf_op jit(solution)/shard_map/cond/branch_3_fun/ppermute | solution.py:185
  120.3 8.5 %collective-permute-start.52 = (f32[1,256]{1,0:T(1,128)S(1)}, f32[1,256]{1,0:T(1,128)S(1)}, u32[]{:S(2)}, u32[]{:S(2)}) collective-permute-start(f32[1,256]{1,0:T(1,128)S(1)} %add.38.refs_5_), channel_id=1, source_target_pairs={{0,1},{1,2},{2,3},{3,0},{4,5},{5,6},{6,7},{7,4},{8,9},{9,10},{10,1... | collective-permute-start | bytes 3080 | tf_op jit(solution)/shard_map/cond/branch_3_fun/ppermute | solution.py:185
  123.1 1.0 copy-start.24
  124.1 4.7 %copy-start.25 = (bf16[1,256,512]{2,1,0:T(8,128)(2,1)S(1)}, bf16[1,256,512]{2,1,0:T(8,128)(2,1)}, u32[]{:S(2)}) copy-start(bf16[1,256,512]{2,1,0:T(8,128)(2,1)} %reduce-scatter.13.cloned.1.call-done) | copy-start | bytes 786436
  124.8 26.2 %collective-permute-start.55 = (bf16[1,512]{1,0:T(2,128)(2,1)}, bf16[1,512]{1,0:T(2,128)(2,1)}, u32[]{:S(2)}, u32[]{:S(2)}) collective-permute-start(bf16[1,512]{1,0:T(2,128)(2,1)} %branch_3_fun.19), channel_id=1, source_target_pairs={{0,448},{8,456},{16,464},{24,472},{32,480},{40,488},{48,496},{56,5... | collective-permute-start | bytes 3080 | tf_op jit(solution)/shard_map/cond/branch_3_fun/ppermute | solution.py:197
Sparse Core Ops, SparseCore 0:
  11.8 44.7 all-gather.18
  60.3 32.5 reduce-scatter.12
